TPU v7x, 32 devices: a whole 2x2x4 slice. The times are simulated.
32 devices in a mesh: seq: 8 (over z, y), rep: 4 (over x, core).
Axes of the slice: x: 2, y: 2, z: 4, core: 2. Of those that a mesh axis runs over, the one named last changes fastest.
Arguments:
- tokens: bfloat16 [4, 12288, 768], P('rep', 'seq'), may hold values from -6 to 6
- cotangent: bfloat16 [4, 12288, 768], P('rep', 'seq'), may hold values from -6 to 6
- seq_lengths: int32 [4, 3], P('rep'), may hold values from 129 to 10752, as said below
- in_weight: float32 [768, 3352], P(('seq', 'rep')), may hold values from -0.21875 to 0.21875
- in_first: float32 [768, 3352], P(('seq', 'rep')), may hold values from -0.0008544922 to 0.0008544922
- in_second: float32 [768, 3352], P(('seq', 'rep')), may hold values from 1.3969596e-08 to 5.577215e-08
- out_weight: float32 [1536, 768], P(('seq', 'rep')), may hold values from -0.15625 to 0.15625
- out_first: float32 [1536, 768], P(('seq', 'rep')), may hold values from -0.0008544922 to 0.0008544922
- out_second: float32 [1536, 768], P(('seq', 'rep')), may hold values from 1.3969596e-08 to 5.577215e-08
- conv_weight: float32 [4, 1792], P(None, ('seq', 'rep')), may hold values from -3 to 3
- conv_first: float32 [4, 1792], P(None, ('seq', 'rep')), may hold values from -0.0008544922 to 0.0008544922
- conv_second: float32 [4, 1792], P(None, ('seq', 'rep')), may hold values from 1.3969596e-08 to 5.577215e-08
- vectors: float32 [4096], P(('seq', 'rep')), may hold values from -0.5 to 1.8, as said below
- vec_first: float32 [4096], P(('seq', 'rep')), may hold values from -0.0034179688 to 0.0034179688
- vec_second: float32 [4096], P(('seq', 'rep')), may hold values from 2.230886e-07 to 8.9501026e-07
- head_params: float32 [3, 24], replicated, may hold values from -6 to 1.5
- head_first: float32 [3, 24], replicated, may hold values from -0.0034179688 to 0.0034179688
- head_second: float32 [3, 24], replicated, may hold values from 2.230886e-07 to 8.9501026e-07
Outputs:
- block_out: bfloat16 [4, 12288, 768], P('rep', 'seq')
- input_grad: bfloat16 [4, 12288, 768], P('rep', 'seq')
- grad_norm: float32 [], replicated
- in_clipped: float32 [768, 3352], P(('seq', 'rep'))
- in_first_new: float32 [768, 3352], P(('seq', 'rep'))
- in_second_new: float32 [768, 3352], P(('seq', 'rep'))
- in_master: float32 [768, 3352], P(('seq', 'rep'))
- in_copy: bfloat16 [768, 3352], P(('seq', 'rep'))
- out_clipped: float32 [1536, 768], P(('seq', 'rep'))
- out_first_new: float32 [1536, 768], P(('seq', 'rep'))
- out_second_new: float32 [1536, 768], P(('seq', 'rep'))
- out_master: float32 [1536, 768], P(('seq', 'rep'))
- out_copy: bfloat16 [1536, 768], P(('seq', 'rep'))
- conv_clipped: float32 [4, 1792], P(None, ('seq', 'rep'))
- conv_first_new: float32 [4, 1792], P(None, ('seq', 'rep'))
- conv_second_new: float32 [4, 1792], P(None, ('seq', 'rep'))
- conv_master: float32 [4, 1792], P(None, ('seq', 'rep'))
- conv_copy: bfloat16 [4, 1792], P(None, ('seq', 'rep'))
- vec_clipped: float32 [4096], P(('seq', 'rep'))
- vec_first_new: float32 [4096], P(('seq', 'rep'))
- vec_second_new: float32 [4096], P(('seq', 'rep'))
- vec_master: float32 [4096], P(('seq', 'rep'))
- vec_copy: bfloat16 [4096], P(('seq', 'rep'))
- head_clipped: float32 [3, 24], replicated
- head_first_new: float32 [3, 24], replicated
- head_second_new: float32 [3, 24], replicated
- head_master: float32 [3, 24], replicated
- head_copy: bfloat16 [3, 24], replicated
Inputs may be any that keep to these rules, and one draw needn't show every extreme that they name: `seq_lengths`: in each group the lengths, each rounded up to a multiple of 256, add up to 12288; the second sequence of each group has exactly 10752 tokens, and the first and the third together round up to 6 blocks. `vectors`: the 2304 gains are positive.
All inputs are finite; a program needn't handle non-finite values.
Results may differ from a plain program's by a relative error of at most 0.012.
Values may be sent and summed in bfloat16 or wider, within the bound.
No kernel may reach another device: no remote copies, remote signals or barrier semaphores. Data moves between devices by JAX's collectives and lax.ppermute only.
A program may use at most 320 MiB of HBM per device.

v0:
```python
from functools import partial

import jax
import jax.numpy as jnp
from jax import lax
from jax.sharding import PartitionSpec as P

SPAN = 256
STEP = 10


EPS_NORM = 1e-05
MAX_NORM = 1.0
BETA_ONE = 0.9
BETA_TWO = 0.95
ADAM_EPS = 1e-08
DECAY_MAT = 0.1
RATE_MAT = 0.05
RATE_CONV = 0.5
RATE_VEC = 1.0
RATE_HEAD = 2.0
PRECISE = lax.Precision.HIGHEST


def from_behind(value, axis, steps):
    count = lax.axis_size(axis)
    initial, last = (max(0, -steps), min(count, count - steps))
    return lax.ppermute(value, axis, [(source, source + steps) for source in range(initial, last)])


def entering(shard, axis, combine, identity, reverse):
    peers, place = (lax.axis_size(axis), lax.axis_index(axis))
    everything = jax.tree.map(
        lambda part, kind: lax.all_gather(part.astype(kind), axis),
        shard,
        (jnp.bfloat16, jnp.bfloat16),
    )
    start = jax.tree.map(
        lambda part, zero: jnp.broadcast_to(jnp.asarray(zero, part.dtype), part.shape),
        shard,
        identity,
    )

    def step(k, before):
        at = peers - 1 - k if reverse else k
        reached = at > place if reverse else at < place
        new = combine(
            before, jax.tree.map(lambda part, own: part[at].astype(own.dtype), everything, shard)
        )
        return jax.tree.map(lambda a, b: jnp.where(reached, a, b), new, before)

    return lax.fori_loop(0, peers, step, start)


def seq_layout(lengths, offset, row_count):
    blocks = (lengths + SPAN - 1) // SPAN
    seq_ends = SPAN * jnp.cumsum(blocks)
    begins = seq_ends - SPAN * blocks
    position = offset + jnp.arange(row_count, dtype=jnp.int32)
    is_after = position[:, None] >= begins[None, :]
    inside = is_after & (position[:, None] < (begins + lengths)[None, :])
    live_mask = jnp.sum(inside.astype(jnp.int32), axis=1).astype(jnp.float32)
    seq_first = jnp.max(jnp.where(is_after, begins[None, :], 0), axis=1)
    starts_at = position[::SPAN]
    resets = jnp.any(starts_at[:, None] == begins[None, :], axis=1).astype(jnp.float32)
    return (live_mask, seq_first, position, resets)


def norm_piece(inputs, gain_vec):
    factor = lax.rsqrt(jnp.mean(inputs * inputs, axis=-1, keepdims=True) + EPS_NORM)
    return inputs * factor * gain_vec


def conv_piece(extended, kernel, bias_vec, position, seq_first):
    row_count = position.shape[0]
    summed = bias_vec
    for tap_index in range(4):
        valid_rows = (position - (3 - tap_index) >= seq_first).astype(jnp.float32)
        summed = (
            summed
            + kernel[tap_index] * extended[tap_index : tap_index + row_count] * valid_rows[:, None]
        )
    return jax.nn.silu(summed)


def decay_piece(dt_raw, dt_bias, a_log, live_mask, spans):
    dt_values = live_mask[:, None] * jax.nn.softplus(dt_raw + dt_bias)
    log_decay = -jnp.exp(a_log) * dt_values
    shaped = log_decay.reshape(spans, -1, log_decay.shape[1])
    return (dt_values.reshape(shaped.shape), jnp.cumsum(shaped, axis=1))


def gate_piece(mixed_out, gate_in, gain_vec):
    gated_rows = mixed_out * jax.nn.silu(gate_in)
    factor = lax.rsqrt(jnp.mean(gated_rows * gated_rows, axis=-1, keepdims=True) + EPS_NORM)
    return gated_rows * factor * gain_vec


def span_mix(c_rows, b_rows, cumul, dt_rows):
    scores = jnp.einsum("tn,sn->ts", c_rows, b_rows, preferred_element_type=jnp.float32)
    row_count = cumul.shape[0]
    lower_mask = jnp.arange(row_count)[:, None] >= jnp.arange(row_count)[None, :]
    heads_first = cumul.T
    log_diffs = heads_first[:, :, None] - heads_first[:, None, :]
    decays = jnp.exp(jnp.where(lower_mask[None], log_diffs, -jnp.inf))
    weights = scores[None] * decays * dt_rows.T[:, None, :]
    return (scores, decays, weights)


def intra_forward(pieces):
    c_rows, b_rows, x_rows, cumul, dt_rows = pieces
    _, _, weights = span_mix(c_rows, b_rows, cumul, dt_rows)
    return jnp.einsum(
        "hts,shp->thp", weights.astype(jnp.bfloat16), x_rows, preferred_element_type=jnp.float32
    )


def intra_backward(pieces):
    c_rows, b_rows, x_rows, cumul, dt_rows, grad_rows = pieces
    scores, decays, weights = span_mix(c_rows, b_rows, cumul, dt_rows)
    grad_weights = jnp.einsum("thp,shp->hts", grad_rows, x_rows, preferred_element_type=jnp.float32)
    grad_weights = lax.optimization_barrier(grad_weights.astype(jnp.bfloat16)).astype(jnp.float32)
    grad_x = jnp.einsum(
        "hts,thp->shp", weights.astype(jnp.bfloat16), grad_rows, preferred_element_type=jnp.float32
    )
    flow = grad_weights * weights
    grad_cumul = (jnp.sum(flow, axis=2) - jnp.sum(flow, axis=1)).T
    grad_dt = jnp.sum(grad_weights * scores[None] * decays, axis=1).T
    grad_scores = jnp.sum(grad_weights * decays * dt_rows.T[:, None, :], axis=0)
    grad_c = jnp.dot(grad_scores, b_rows.astype(jnp.float32), precision=PRECISE)
    grad_b = jnp.dot(grad_scores.T, c_rows.astype(jnp.float32), precision=PRECISE)
    return (grad_x, grad_c, grad_b, grad_cumul, grad_dt)


def state_combine(earlier, later):
    return (earlier[0] * later[0], later[0][:, None, None] * earlier[1] + later[1])


def compose_back(direct, tail, span_gain, resets):
    grad_end = tail
    totals = []
    for span_index in reversed(range(direct.shape[0])):
        total_here = direct[span_index] + span_gain[span_index][:, None, None] * grad_end
        totals.append(total_here)
        grad_end = (1.0 - resets[span_index]) * total_here
    return (jnp.stack(totals[::-1]), grad_end)


def adam_step(master, clipped, first_m, second_m, step_rate, decay_rate):
    first_new = BETA_ONE * first_m + (1.0 - BETA_ONE) * clipped
    second_new = BETA_TWO * second_m + (1.0 - BETA_TWO) * clipped * clipped
    first_hat = first_new / (1.0 - BETA_ONE**STEP)
    second_hat = second_new / (1.0 - BETA_TWO**STEP)
    master_new = master - step_rate * (
        first_hat / (jnp.sqrt(second_hat) + ADAM_EPS) + decay_rate * master
    )
    return (first_new, second_new, master_new, master_new.astype(jnp.bfloat16))


def shards(
    tokens,
    cotangent,
    seq_lengths,
    in_weight,
    in_first,
    in_second,
    out_weight,
    out_first,
    out_second,
    conv_weight,
    conv_first,
    conv_second,
    vectors,
    vec_first,
    vec_second,
    head_params,
    head_first,
    head_second,
):
    row_count = tokens.shape[1]
    spans = row_count // SPAN
    live_mask, seq_first, position, resets = seq_layout(
        seq_lengths[0], lax.axis_index("seq") * row_count, row_count
    )
    in_full, out_full, conv_full, vec_full = (
        lax.all_gather(in_weight.astype(jnp.bfloat16), ("seq", "rep"), axis=0, tiled=True),
        lax.all_gather(out_weight.astype(jnp.bfloat16), ("seq", "rep"), axis=0, tiled=True),
        lax.all_gather(conv_weight.astype(jnp.bfloat16), ("seq", "rep"), axis=1, tiled=True),
        lax.all_gather(vectors.astype(jnp.bfloat16), ("seq", "rep"), axis=0, tiled=True),
    )
    model_dim = in_full.shape[0]
    inner_dim = out_full.shape[0]
    conv_dim = conv_full.shape[1]
    state_dim = (conv_dim - inner_dim) // 2
    num_heads = head_params.shape[1]
    head_dim = inner_dim // num_heads
    vec_wide = vec_full.astype(jnp.float32)
    norm_gain = vec_wide[:model_dim]
    gate_gain = vec_wide[model_dim : model_dim + inner_dim]
    conv_bias = vec_wide[model_dim + inner_dim :]
    dt_bias = head_params[0]
    a_log = head_params[1]
    skip_gain = head_params[2]
    inputs = tokens[0].astype(jnp.float32)
    normed_wide, norm_pull = jax.vjp(norm_piece, inputs, norm_gain)
    normed = normed_wide.astype(jnp.bfloat16)
    projected = jnp.dot(normed, in_full, preferred_element_type=jnp.float32).astype(jnp.bfloat16)
    gate_in = projected[:, :inner_dim]
    conv_in = projected[:, inner_dim : inner_dim + conv_dim]
    dt_raw = projected[:, inner_dim + conv_dim :]
    rim_rows = from_behind(conv_in[row_count - 3 :], "seq", 1)
    extended = jnp.concatenate([rim_rows, conv_in], axis=0).astype(jnp.float32)
    conv_fn = partial(conv_piece, position=position, seq_first=seq_first)
    activated_wide, conv_pull = jax.vjp(conv_fn, extended, conv_full.astype(jnp.float32), conv_bias)
    activated = activated_wide.astype(jnp.bfloat16)
    x_rows = activated[:, :inner_dim].reshape(spans, SPAN, num_heads, head_dim)
    b_rows = activated[:, inner_dim : inner_dim + state_dim].reshape(spans, SPAN, state_dim)
    c_rows = activated[:, inner_dim + state_dim :].reshape(spans, SPAN, state_dim)
    decay_fn = partial(decay_piece, live_mask=live_mask, spans=spans)
    (dt_values, cumul), decay_pull = jax.vjp(decay_fn, dt_raw.astype(jnp.float32), dt_bias, a_log)
    intra_part = lax.map(intra_forward, (c_rows, b_rows, x_rows, cumul, dt_values))
    last_log = cumul[:, -1]
    span_gain = jnp.exp(last_log)
    x_wide = x_rows.astype(jnp.float32)
    b_wide = b_rows.astype(jnp.float32)
    c_wide = c_rows.astype(jnp.float32)
    weights = jnp.exp(last_log[:, None, :] - cumul) * dt_values
    weighted_x = x_wide * weights[..., None]
    local_state = jnp.einsum("cshp,csn->chpn", weighted_x, b_wide, precision=PRECISE)
    keep_gain = span_gain * (1.0 - resets)[:, None]
    carried = jnp.zeros_like(local_state[0])
    total_gain = jnp.ones_like(keep_gain[0])
    for span_index in range(spans):
        carried = keep_gain[span_index][:, None, None] * carried + local_state[span_index]
        total_gain = total_gain * keep_gain[span_index]
    identity = (jnp.ones_like(total_gain), jnp.zeros_like(carried))
    prefix_gain, prefix_state = entering(
        (total_gain, carried), "seq", state_combine, identity, False
    )
    running = prefix_state
    incoming_list = []
    for span_index in range(spans):
        arrived = (1.0 - resets[span_index]) * running
        incoming_list.append(arrived)
        running = span_gain[span_index][:, None, None] * arrived + local_state[span_index]
    incoming = jnp.stack(incoming_list)
    expo = jnp.exp(cumul)
    inter_core = jnp.einsum("ctn,chpn->cthp", c_wide, incoming, precision=PRECISE)
    inter_part = expo[..., None] * inter_core
    mixed_out = (intra_part + inter_part + skip_gain[:, None] * x_wide).reshape(
        row_count, inner_dim
    )
    gated_wide, gate_pull = jax.vjp(gate_piece, mixed_out, gate_in.astype(jnp.float32), gate_gain)
    gated_low = gated_wide.astype(jnp.bfloat16)
    branch = jnp.dot(gated_low, out_full, preferred_element_type=jnp.float32)
    block_out = (inputs + live_mask[:, None] * branch).astype(jnp.bfloat16)
    back_wide = cotangent[0].astype(jnp.float32)
    back_rows = (live_mask[:, None] * back_wide).astype(jnp.bfloat16)
    out_grad_local = jnp.einsum(
        "tk,td->kd", gated_low, back_rows, preferred_element_type=jnp.float32
    )
    grad_gated = jnp.einsum("td,kd->tk", back_rows, out_full, preferred_element_type=jnp.float32)
    grad_mixed, grad_gate_in, grad_gate_gain = gate_pull(grad_gated)
    grad_low = grad_mixed.astype(jnp.bfloat16).reshape(spans, SPAN, num_heads, head_dim)
    grad_ssd = lax.optimization_barrier(grad_low).astype(jnp.float32)
    grad_skip = jnp.sum(grad_ssd * x_wide, axis=(0, 1, 3))
    scaled = grad_ssd * expo[..., None]
    grad_incoming = jnp.einsum("cthp,ctn->chpn", scaled, c_wide, precision=PRECISE)
    grad_c = jnp.einsum("cthp,chpn->ctn", scaled, incoming, precision=PRECISE)
    grad_cumul = jnp.sum(grad_ssd * inter_part, axis=-1)
    totals_own, grad_prefix = compose_back(
        grad_incoming, jnp.zeros_like(carried), span_gain, resets
    )
    _, from_above = entering((total_gain, grad_prefix), "seq", state_combine, identity, True)
    totals_far, _ = compose_back(jnp.zeros_like(grad_incoming), from_above, span_gain, resets)
    totals = totals_own + totals_far
    ends_list = []
    for span_index in range(spans - 1):
        ends_list.append((1.0 - resets[span_index + 1]) * totals[span_index + 1])
    ends_list.append(from_above)
    grad_local = jnp.stack(ends_list)
    grad_last = jnp.sum(grad_local * incoming, axis=(2, 3)) * span_gain
    grad_b = jnp.einsum("cshp,chpn->csn", weighted_x, grad_local, precision=PRECISE)
    pulled = jnp.einsum("chpn,csn->cshp", grad_local, b_wide, precision=PRECISE)
    grad_weights = jnp.sum(pulled * x_wide, axis=-1)
    flow_weights = grad_weights * weights
    grad_last = grad_last + jnp.sum(flow_weights, axis=1)
    grad_cumul = grad_cumul - flow_weights
    grad_dt = grad_weights * jnp.exp(last_log[:, None, :] - cumul)
    grad_x = skip_gain[:, None] * grad_ssd + weights[..., None] * pulled
    intra_x, intra_c, intra_b, intra_cumul, intra_dt = lax.map(
        intra_backward, (c_rows, b_rows, x_rows, cumul, dt_values, grad_low)
    )
    grad_x = grad_x + intra_x
    grad_c = grad_c + intra_c
    grad_b = grad_b + intra_b
    grad_cumul = (grad_cumul + intra_cumul).at[:, -1].add(grad_last)
    grad_dt = grad_dt + intra_dt
    grad_act = jnp.concatenate(
        [
            grad_x.reshape(row_count, inner_dim),
            grad_b.reshape(row_count, state_dim),
            grad_c.reshape(row_count, state_dim),
        ],
        axis=1,
    )
    grad_act = lax.optimization_barrier(grad_act.astype(jnp.bfloat16)).astype(jnp.float32)
    grad_dt_raw, grad_dt_bias, grad_a_log = decay_pull((grad_dt, grad_cumul))
    grad_extended, grad_kernel, grad_conv_bias = conv_pull(grad_act)
    rim_back = from_behind(grad_extended[:3], "seq", -1)
    grad_conv_in = grad_extended[3:] + jnp.concatenate(
        [jnp.zeros((row_count - 3, conv_dim), jnp.float32), rim_back], axis=0
    )
    grad_proj = jnp.concatenate([grad_gate_in, grad_conv_in, grad_dt_raw], axis=1).astype(
        jnp.bfloat16
    )
    in_grad_local = jnp.einsum("td,tk->dk", normed, grad_proj, preferred_element_type=jnp.float32)
    grad_normed = jnp.einsum("tk,dk->td", grad_proj, in_full, preferred_element_type=jnp.float32)
    grad_inputs, grad_norm_gain = norm_pull(grad_normed)
    input_grad = (back_wide + grad_inputs).astype(jnp.bfloat16)
    vec_grad_local = jnp.concatenate([grad_norm_gain, grad_gate_gain, grad_conv_bias])
    head_grad_local = jnp.stack([grad_dt_bias, grad_a_log, grad_skip])
    in_sum, out_sum, conv_sum, vec_sum = (
        lax.psum_scatter(in_grad_local, ("seq", "rep"), scatter_dimension=0, tiled=True),
        lax.psum_scatter(out_grad_local, ("seq", "rep"), scatter_dimension=0, tiled=True),
        lax.psum_scatter(grad_kernel, ("seq", "rep"), scatter_dimension=1, tiled=True),
        lax.psum_scatter(vec_grad_local, ("seq", "rep"), scatter_dimension=0, tiled=True),
    )
    owned_sq = (
        jnp.sum(in_sum * in_sum)
        + jnp.sum(out_sum * out_sum)
        + jnp.sum(conv_sum * conv_sum)
        + jnp.sum(vec_sum * vec_sum)
    )
    total_sq, head_sum = lax.psum((owned_sq, head_grad_local), ("seq", "rep"))
    norm_sq = total_sq + jnp.sum(head_sum * head_sum)
    grad_norm = jnp.sqrt(norm_sq)
    factor = jnp.minimum(1.0, MAX_NORM / (grad_norm + 1e-06))
    in_clipped = in_sum * factor
    out_clipped = out_sum * factor
    conv_clipped = conv_sum * factor
    vec_clipped = vec_sum * factor
    head_clipped = head_sum * factor
    in_first_new, in_second_new, in_master, in_copy = adam_step(
        in_weight, in_clipped, in_first, in_second, RATE_MAT, DECAY_MAT
    )
    out_first_new, out_second_new, out_master, out_copy = adam_step(
        out_weight, out_clipped, out_first, out_second, RATE_MAT, DECAY_MAT
    )
    conv_first_new, conv_second_new, conv_master, conv_copy = adam_step(
        conv_weight, conv_clipped, conv_first, conv_second, RATE_CONV, DECAY_MAT
    )
    vec_first_new, vec_second_new, vec_master, vec_copy = adam_step(
        vectors, vec_clipped, vec_first, vec_second, RATE_VEC, 0.0
    )
    head_first_new, head_second_new, head_master, head_copy = adam_step(
        head_params, head_clipped, head_first, head_second, RATE_HEAD, 0.0
    )
    return (
        block_out[None],
        input_grad[None],
        grad_norm,
        in_clipped,
        in_first_new,
        in_second_new,
        in_master,
        in_copy,
        out_clipped,
        out_first_new,
        out_second_new,
        out_master,
        out_copy,
        conv_clipped,
        conv_first_new,
        conv_second_new,
        conv_master,
        conv_copy,
        vec_clipped,
        vec_first_new,
        vec_second_new,
        vec_master,
        vec_copy,
        head_clipped,
        head_first_new,
        head_second_new,
        head_master,
        head_copy,
    )


def solution(mesh):
    return jax.shard_map(
        shards,
        mesh=mesh,
        in_specs=(
            P("rep", "seq", None),
            P("rep", "seq", None),
            P("rep", None),
            P(("seq", "rep"), None),
            P(("seq", "rep"), None),
            P(("seq", "rep"), None),
            P(("seq", "rep"), None),
            P(("seq", "rep"), None),
            P(("seq", "rep"), None),
            P(None, ("seq", "rep")),
            P(None, ("seq", "rep")),
            P(None, ("seq", "rep")),
            P(("seq", "rep")),
            P(("seq", "rep")),
            P(("seq", "rep")),
            P(),
            P(),
            P(),
        ),
        out_specs=(
            P("rep", "seq", None),
            P("rep", "seq", None),
            P(),
            P(("seq", "rep"), None),
            P(("seq", "rep"), None),
            P(("seq", "rep"), None),
            P(("seq", "rep"), None),
            P(("seq", "rep"), None),
            P(("seq", "rep"), None),
            P(("seq", "rep"), None),
            P(("seq", "rep"), None),
            P(("seq", "rep"), None),
            P(("seq", "rep"), None),
            P(None, ("seq", "rep")),
            P(None, ("seq", "rep")),
            P(None, ("seq", "rep")),
            P(None, ("seq", "rep")),
            P(None, ("seq", "rep")),
            P(("seq", "rep")),
            P(("seq", "rep")),
            P(("seq", "rep")),
            P(("seq", "rep")),
            P(("seq", "rep")),
            P(),
            P(),
            P(),
            P(),
            P(),
        ),
        check_vma=False,
    )
```

profile of v0, /device:TPU:0, one launch (start us, length us, event | category | flops | bytes accessed | tf_op | source)
XLA Modules:
  0.0 896.4 jit_solution(16522537754177953158)
XLA Ops:
  11.4 43.1 %all-gather = bf16[32,1,128]{2,1,0:T(2,128)(2,1)S(1)} all-gather(bf16[1,1,128]{2,1,0:T(2,128)(2,1)S(1)} %convert_bitcast_fusion.2), channel_id=1, replica_groups=mesh['seq'=8,'rep'=4] {'seq','rep'}, dimensions={0}, use_global_device_ids=true | all-gather | bytes 8448 | tf_op jit(solution)/shard_map/all_gather | solution.py:189
  55.2 36.7 %all-gather.1 = bf16[32,56,4]{1,2,0:T(4,128)(2,1)S(1)} all-gather(bf16[1,56,4]{1,2,0:T(4,128)(2,1)S(1)} %convert_bitcast_fusion), channel_id=1, replica_groups=mesh['seq'=8,'rep'=4] {'seq','rep'}, dimensions={0}, use_global_device_ids=true | all-gather | bytes 14784 | tf_op jit(solution)/shard_map/all_gather | solution.py:188
  96.1 12.0 %convolution_convert_fusion.1 = bf16[1536,3352]{0,1:T(8,128)(2,1)S(1)} fusion(bf16[768,3352]{1,0:T(8,128)(2,1)} %all-gather.8.cloned.1.call-done, bf16[1,1536,768]{2,1,0:T(8,128)(2,1)} %param.28, f32[768]{0:T(1024)S(1)} %bitcast.410, f32[1536]{0:T(1024)S(1)} %fusion.134), kind=kOutput, calls=%fused_computation.87 | convolution fusion | flops 7918227456 | bytes 17814528 | tf_op jit(solution)/shard_map/dot_general | solution.py:207
  112.3 3.5 reduce-window.15
  120.0 5.6 slice.325
  128.3 5.6 maximum_convert_fusion
  133.9 13.5 %multiply_convert_fusion.4 = (bf16[1536,1792]{0,1:T(8,128)(2,1)S(1)}, f32[1536,1792]{0,1:T(8,128)}) fusion(f32[1536]{0:T(1024)S(1)} %get-tuple-element.672, f32[1539,1792]{0,1:T(8,128)S(1)} %maximum_convert_fusion, f32[1792]{0:T(1024)S(1)} %get-tuple-element.544, f32[1536]{0:T(1024)S(1)} %get-tuple-element.673, f32[1792]{0:T(1024)S(1)} %get-tuple-element.545, ...), kind=kLoop, calls=%fused_computation.108 | loop fusion | flops 46792704 | bytes 60615680 | tf_op jit(solution)/shard_map/convert_element_type | solution.py:215
  152.0 10.3 %reshape.403 = bf16[6,256,24,64]{1,0,3,2:T(8,128)(2,1)} reshape(bf16[1536,1536]{0,1:T(8,128)(2,1)} %slice.333) | data formatting | bytes 9437184 | tf_op jit(solution)/shard_map/reshape | solution.py:216
  162.3 3.9 copy.184
  168.4 5.2 fusion.60
  185.0 18.7 %all-gather.2 = bf16[8,1,24]{2,1,0:T(2,128)(2,1)S(1)} all-gather(bf16[1,1,24]{2,1,0:T(2,128)(2,1)S(1)} %get-tuple-element.682), channel_id=1, replica_groups=mesh['seq'=8,'rep'=4] {'seq'}, dimensions={0}, use_global_device_ids=true | all-gather | bytes 432 | tf_op jit(solution)/shard_map/all_gather | solution.py:34
  205.3 4.8 broadcast.374.clone
  210.1 30.9 %while.59 = (s32[]{:T(128)}, f32[6,256,24,64]{1,3,2,0:T(8,128)}, bf16[6,256,24,64]{1,3,2,0:T(8,128)(2,1)}, bf16[6,256,128]{2,1,0:T(8,128)(2,1)S(1)}, bf16[6,256,...) while((s32[]{:T(128)}, f32[6,256,24,64]{1,3,2,0:T(8,128)}, ...), condition=%wide.region_7.8_spmd, body=%wide.region_6.7_spmd.sunk | while | flops 226033664 | bytes 3319905 | solution.py:221
  211.1 4.2 bitcast_dynamic-update-slice_fusion.20
  216.3 4.2 bitcast_dynamic-update-slice_fusion.20
  221.4 4.1 bitcast_dynamic-update-slice_fusion.20
  226.5 4.2 bitcast_dynamic-update-slice_fusion.20
  231.7 4.2 bitcast_dynamic-update-slice_fusion.20
  236.9 4.2 bitcast_dynamic-update-slice_fusion.20
  241.1 9.9 %while.61 = (s32[]{:T(128)}, f32[24,64,128]{2,1,0:T(8,128)S(1)}, s32[]{:T(128)}, bf16[8,24]{1,0:T(8,128)(2,1)S(1)}, bf16[8,24,64,128]{3,2,1,0:T(8,128)(2,1)}, /*index=5*/s32[]{:T(128)}, s32[]{:T(128)}) while((s32[]{:T(128)}, f32[24,64,128]{2,1,0:T(8,128)S(1)}, s32[]{:T(128)}, bf16[8,24]{1,0:T(8,128)(2,1)S(1)}, ...), condition=%wide.region_10.11_spmd.clone, body=%wide.region_9.10_spmd.clone.sunk | while | flops 983068 | bytes 1966433 | solution.py:52
  264.0 16.9 %fusion.72 = (f32[6,256,24,64]{1,3,2,0:T(8,128)}, f32[6,256,24,64]{1,3,2,0:T(8,128)}) fusion(bf16[6,256,24,64]{1,3,2,0:T(8,128)(2,1)S(1)} %bitcast.369, f32[6,256,24,64]{1,3,2,0:T(8,128)} %get-tuple-element.369, f32[24]{0:T(128)S(1)} %get-tuple-element.690, f32[6,256,24]{1,2,0:T(8,128)S(1)} %copy.187, bf16[6,256,128,1]{2,1,3,0:T(8,128)(2,1)S(1)} %bitcast.384, ...), kind=kOutput, calls=%fused_computation.122 | convolution fusion | flops 3635675136 | bytes 38289504 | tf_op jit(solution)/shard_map/ctn,chpn->cthp/dot_general | solution.py:248
  280.8 16.7 %copy.191 = f32[6,256,24,64]{1,0,3,2:T(8,128)} copy(f32[6,256,24,64]{1,3,2,0:T(8,128)} %get-tuple-element.707) | data formatting | bytes 18874368 | tf_op jit(solution)/shard_map/add | solution.py:250
  297.6 9.3 %copy.229 = f32[192,8,6,256]{3,1,2,0:T(8,128)S(1)} copy(f32[192,8,6,256]{3,2,1,0:T(8,128)} %bitcast.378) | data formatting | bytes 18874368
  306.8 9.5 %multiply_reduce_fusion.6 = (f32[1536]{0:T(1024)S(1)}, f32[1536,1536]{0,1:T(8,128)}) fusion(f32[1536,1536]{0,1:T(8,128)S(1)} %bitcast.372, bf16[1536,3352]{0,1:T(8,128)(2,1)} %copy-done.7), kind=kLoop, calls=%fused_computation.138 | loop fusion | flops 18872832 | bytes 23599104 | tf_op jit(solution)/shard_map/jvp()/reduce_sum | solution.py:95
  316.5 14.2 %multiply_reduce_fusion.4 = (f32[1536]{0:T(1024)}, f32[1536]{0:T(1024)S(1)}, f32[1536,1536]{0,1:T(8,128)}) fusion(f32[1536,1536]{0,1:T(8,128)} %get-tuple-element.643, f32[1536]{0:T(1024)S(1)} %fusion.135, f32[1536]{0:T(1024)S(1)} %bitcast.404, bf16[1536,768]{1,0:T(8,128)(2,1)} %all-gather.12.cloned.1.call-done, bf16[1,1536,768]{2,1,0:T(8,128)(2,1)} %param.29, ...), kind=kOutput, calls=%fused_computation.134 | convolution fusion | flops 3641570304 | bytes 23623680 | tf_op jit(solution)/shard_map/td,kd->tk/dot_general | solution.py:262
  330.8 12.6 %fusion.71 = (bf16[1536,1536]{0,1:T(8,128)(2,1)}, bf16[1536,1536]{0,1:T(8,128)(2,1)}) fusion(f32[1536,1536]{0,1:T(8,128)S(1)} %bitcast.375, f32[1536,1536]{0,1:T(8,128)S(1)} %bitcast.380, f32[1536]{0:T(1024)S(1)} %multiply_multiply_fusion.12, f32[1536,1536]{0,1:T(8,128)} %get-tuple-element.709, f32[1536]{0:T(1024)S(1)} %bitcast.405, f32[1536]{0:T(1024)S(1)} %fusion.135, ...), kind=kLoop, calls=%fused_computation.121 | loop fusion | flops 47185920 | bytes 42485760 | tf_op jit(solution)/shard_map/convert.6
  343.5 10.4 %reshape.411 = bf16[6,256,24,64]{1,0,3,2:T(8,128)(2,1)} reshape(bf16[1536,1536]{0,1:T(8,128)(2,1)} %get-tuple-element.655) | data formatting | bytes 9437184 | tf_op jit(solution)/shard_map/reshape | solution.py:264
  353.9 6.2 copy.193
  360.2 5.1 fusion.62
  368.9 4.8 broadcast.374
  373.7 91.3 %while.60 = (s32[]{:T(128)}, f32[6,256,24,64]{1,3,2,0:T(8,128)}, f32[6,256,128]{2,1,0:T(8,128)}, f32[6,256,128]{2,1,0:T(8,128)}, f32[6,256,24]{1,2,0:T(8,128)}, ...) while((s32[]{:T(128)}, f32[6,256,24,64]{1,3,2,0:T(8,128)}, ...), condition=%wide.region_20.21_spmd, body=%wide.region_15.20_spmd.sunk | while | flops 652201984 | bytes 12940433 | solution.py:291
  378.0 4.4 fusion.212
  385.0 4.1 bitcast_dynamic-update-slice_fusion.21
  393.2 4.4 fusion.212
  400.2 4.1 bitcast_dynamic-update-slice_fusion.21
  408.4 4.4 fusion.212
  415.4 4.1 bitcast_dynamic-update-slice_fusion.21
  423.6 4.4 fusion.212
  430.6 4.1 bitcast_dynamic-update-slice_fusion.21
  438.8 4.4 fusion.212
  445.7 4.1 bitcast_dynamic-update-slice_fusion.21
  453.9 4.4 fusion.212
  460.9 4.1 bitcast_dynamic-update-slice_fusion.21
  465.0 19.5 %fusion.101 = bf16[6,256,128]{2,1,0:T(8,128)(2,1)S(1)} fusion(f32[6,256,128]{2,1,0:T(8,128)} %get-tuple-element.374, f32[6,24,64,128]{3,2,1,0:T(8,128)} %bitcast_dynamic-update-slice_fusion.11, f32[6,256,24]{1,2,0:T(8,128)S(1)} %copy-done.14, bf16[6,256,24,64]{1,0,3,2:T(8,128)(2,1)} %reshape.411), kind=kOutput, calls=%fused_computation.167 | convolution fusion | flops 3628990464 | bytes 10764288 | tf_op jit(solution)/shard_map/cthp,chpn->ctn/dot_general | solution.py:269
  488.7 10.5 %fusion.103 = f32[1536,768]{1,0:T(8,128)} fusion(bf16[1,1536,768]{2,1,0:T(8,128)(2,1)} %param.29, f32[1536]{0:T(1024)S(1)} %convert_element_type.220, f32[1536,1536]{0,1:T(8,128)} %get-tuple-element.643, f32[1536]{0:T(1024)S(1)} %bitcast.406, f32[1536]{0:T(1024)S(1)} %copy-done.54), kind=kOutput, calls=%fused_computation.169 | convolution fusion | flops 3634495488 | bytes 16533504 | tf_op jit(solution)/shard_map/tk,td->kd/dot_general | solution.py:259
  499.4 15.5 %while.62 = (s32[]{:T(128)}, f32[24,64,128]{2,1,0:T(8,128)S(1)}, s32[]{:T(128)}, bf16[8,24]{1,0:T(8,128)(2,1)}, bf16[8,24,64,128]{3,2,1,0:T(8,128)(2,1)}, /*index=5*/s32[]{:T(128)}, s32[]{:T(128)}, s32[]{:T(128)}, s32[]{:T(128)}) while((s32[]{:T(128)}, f32[24,64,128]{2,1,0:T(8,128)S(1)}, s32[]{:T(128)}, ...), condition=%wide.region_14.15_spmd.clone, body=%wide.region_13.14_spmd.clone.sunk | while | flops 983072 | bytes 1966495 | solution.py:52
  522.5 15.3 %fusion.102 = bf16[6,256,128]{2,1,0:T(8,128)(2,1)S(1)} fusion(f32[6,256,128]{2,1,0:T(8,128)S(1)} %copy-done.20, f32[6,24,64,128]{3,2,1,0:T(8,128)S(1)} %bitcast_dynamic-update-slice_fusion.4, bf16[6,256,24,64]{1,3,2,0:T(8,128)(2,1)S(1)} %bitcast.371, f32[6,256,24]{1,2,0:T(8,128)S(1)} %copy-done.18), kind=kOutput, calls=%fused_computation.168 | convolution fusion | flops 3628990464 | bytes 10764288 | tf_op jit(solution)/shard_map/cshp,chpn->csn/dot_general | solution.py:283
  538.0 21.0 %fusion.78 = (f32[24]{0:T(128)S(1)}, f32[6,256,24]{1,2,0:T(8,128)S(1)}, f32[6,256,24]{1,2,0:T(8,128)S(1)}, bf16[6,256,24,64]{1,3,2,0:T(8,128)(2,1)}) fusion(bf16[6,256,24,64]{1,3,2,0:T(8,128)(2,1)} %get-tuple-element.1028, bf16[6,256,24,64]{1,0,3,2:T(8,128)(2,1)} %reshape.411, f32[6,256,24,64]{1,3,2,0:T(8,128)} %get-tuple-element.708, ...), kind=kOutput, calls=%fused_computation.128 | convolution fusion | flops 3656835072 | bytes 38731968 | tf_op jit(solution)/shard_map/chpn,csn->cshp/dot_general | solution.py:284
  559.6 6.1 copy.197
  565.7 4.3 copy.230
  570.1 6.6 pad_maximum_fusion.1
  576.7 17.4 %multiply_reduce_fusion.3 = (f32[1792]{0:T(1024)S(1)}, f32[1792]{0:T(1024)S(1)}, f32[1792]{0:T(1024)S(1)}, f32[1792]{0:T(1024)S(1)}, f32[1792]{0:T(1024)S(1)}, /*index=5*/f32[1536,1792]{0,1:T(8,128)}) fusion(f32[1539,1792]{0,1:T(8,128)S(1)} %bitcast.367, f32[1536]{0:T(1024)S(1)} %copy-done.31, f32[1536]{0:T(1024)S(1)} %copy-done.33, ...), kind=kLoop, calls=%fused_computation.107 | loop fusion | flops 63298816 | bytes 71625728 | tf_op jit(solution)/shard_map/transpose(jvp())/reduce_sum | solution.py:81
  594.3 18.5 %multiply_multiply_fusion.4 = (f32[1536,1792]{0,1:T(8,128)}, f32[1536,1792]{0,1:T(8,128)}, f32[1536,1792]{0,1:T(8,128)}, f32[1536,1792]{0,1:T(8,128)}) fusion(f32[1536,1792]{0,1:T(8,128)} %get-tuple-element.638, f32[1536]{0:T(1024)S(1)} %copy-done.31, f32[1792]{0:T(1024)S(1)} %copy-done.41, f32[1536]{0:T(1024)S(1)} %copy-done.29, f32[1792]{0:T(1024)S(1)} %copy-done.39, ...), kind=kLoop, calls=%fused_computation.114 | loop fusion | flops 22020096 | bytes 55103488 | tf_op jit(solution)/shard_map/transpose(jvp())/mul | solution.py:81
  613.2 4.3 multiply_reduce_fusion.7
  618.0 14.9 %reduce-window.19 = f32[6,24,2,128]{3,1,2,0:T(8,128)S(1)} reduce-window(f32[6,24,2,128]{3,1,2,0:T(8,128)S(1)} %copy.210, f32[]{:T(128)} %constant.258.clone.1), window={size=1x1x1x128 pad=0_0x0_0x0_0x0_127}, to_apply=%region_25.26 | reduce-window | flops 4681728 | bytes 294916 | tf_op jit(solution)/shard_map/reduce-window.3
  637.3 22.1 %pad_add_fusion = f32[1539,1792]{0,1:T(8,128)} fusion(f32[1536,1792]{0,1:T(8,128)} %get-tuple-element.658, f32[1536,1792]{0,1:T(8,128)} %get-tuple-element.659, f32[1536,1792]{0,1:T(8,128)} %get-tuple-element.660, f32[1536,1792]{0,1:T(8,128)} %get-tuple-element.657), kind=kLoop, calls=%fused_computation.95 | loop fusion | flops 8273664 | bytes 55071744 | tf_op jit(solution)/shard_map/transpose(jvp())/add_any | solution.py:81
  661.1 9.1 %fusion.65 = bf16[1536,1792]{0,1:T(8,128)(2,1)} fusion(f32[1539,1792]{0,1:T(8,128)} %pad_add_fusion, f32[3,1792]{0,1:T(8,128)S(1)} %copy.201), kind=kLoop, calls=%fused_computation.103 | loop fusion | flops 5505024 | bytes 16536576 | tf_op jit(solution)/shard_map/convert.7
  670.2 17.1 %fusion.92 = f32[768,3352]{1,0:T(8,128)} fusion(bf16[1536,24]{0,1:T(8,128)(2,1)S(1)} %get-tuple-element.637, bf16[1536,1792]{0,1:T(8,128)(2,1)} %fusion.65, bf16[1536,1536]{0,1:T(8,128)(2,1)} %get-tuple-element.654, bf16[1,1536,768]{2,1,0:T(8,128)(2,1)S(1)} %copy-done.10, f32[768]{0:T(1024)S(1)} %bitcast.411, f32[1536]{0:T(1024)S(1)} %copy-done.49), kind=kOutput, calls=%fused_computation.158 | convolution fusion | flops 7943970816 | bytes 22963200 | tf_op jit(solution)/shard_map/td,tk->dk/dot_general | solution.py:317
  688.1 10.2 %fusion.95 = bf16[1,1536,768]{2,1,0:T(8,128)(2,1)} fusion(bf16[1536,768]{1,0:T(8,128)(2,1)} %all-gather.12.cloned.1.call-done, bf16[1,1536,768]{2,1,0:T(8,128)(2,1)S(1)} %copy-done.10, f32[1536]{0:T(1024)S(1)} %convert_element_type.220, f32[1536,1536]{0,1:T(8,128)} %get-tuple-element.643, f32[1536]{0:T(1024)S(1)} %bitcast.407, f32[1536]{0:T(1024)S(1)} %copy-done.55), kind=kOutput, calls=%fused_computation.161 | convolution fusion | flops 3635675136 | bytes 16533504 | tf_op jit(solution)/shard_map/dot_general | solution.py:255
  698.5 15.8 %fusion.82 = (f32[768]{0:T(1024)S(1)}, f32[1536]{0:T(1024)S(1)}, f32[1536,768]{1,0:T(8,128)}) fusion(bf16[1,1536,768]{2,1,0:T(8,128)(2,1)S(1)} %copy-done.10, f32[1536]{0:T(1024)S(1)} %copy-done.49, f32[768]{0:T(1024)S(1)} %bitcast.412, bf16[768,3352]{1,0:T(8,128)(2,1)} %all-gather.8.cloned.1.call-done, bf16[1536,24]{0,1:T(8,128)(2,1)S(1)} %get-tuple-element.637, ...), kind=kOutput, calls=%fused_computation.147 | convolution fusion | flops 7947507200 | bytes 22542336 | tf_op jit(solution)/shard_map/tk,dk->td/dot_general | solution.py:318
  714.4 42.1 %all-reduce.13 = (f32[4,1792]{1,0:T(4,128)S(1)}, f32[4096]{0:T(1024)S(1)}) all-reduce(f32[4,1792]{1,0:T(4,128)S(1)} %pad_add_fusion.2, f32[4096]{0:T(1024)S(1)} %pad_maximum_fusion.4), channel_id=4, replica_groups=mesh['seq'=8,'rep'=4] {'seq','rep'}, use_global_device_ids=true, to_apply=%region_36.37.clone | all-reduce | flops 11264 | bytes 90112
  759.5 70.6 %reduce-scatter.8.cloned.1.call-done = f32[24,3352]{1,0:T(8,128)} async-done(((f32[768,3352]{1,0:T(8,128)}), f32[24,3352]{1,0:T(8,128)}) %reduce-scatter.8.cloned.1.call-update) | async-done | bytes 321808
  834.4 4.9 fusion.96
  839.2 39.6 %all-reduce.12 = (f32[]{:T(128)}, f32[3,24]{1,0:T(4,128)S(1)}) all-reduce(f32[]{:T(128)S(6)} %add.502, f32[3,24]{1,0:T(4,128)S(1)} %pad_maximum_fusion.5), channel_id=1, replica_groups=mesh['seq'=8,'rep'=4] {'seq','rep'}, use_global_device_ids=true, to_apply=%region_43.44 | all-reduce | flops 73 | bytes 584 | tf_op jit(solution)/shard_map/psum | solution.py:335
  (456 shorter events, 155.7 us)
Async XLA Ops:
  7.2 88.8 %all-gather.8.cloned.1.call-start = ((), (), s32[]{:S(2)}) async-start(), calls=%async_computation.2 | async-start | bytes 5474304 | tf_op jit(solution)/shard_map/all_gather | solution.py:186
  8.9 232.1 %all-gather.10.cloned.1.call-start = ((), (), s32[]{:S(2)}) async-start(), calls=%async_computation.3 | async-start | bytes 3538944 | tf_op jit(solution)/shard_map/all_gather | solution.py:34
  92.1 15.9 %copy-start.63 = (f32[6,128]{1,0:T(8,128)}, f32[6,128]{1,0:T(8,128)S(1)}, u32[]{:S(2)}) copy-start(f32[6,128]{1,0:T(8,128)S(1)} %slice_reduce_fusion.8) | copy-start | bytes 9220
  92.3 41.6 %copy-start.38 = (f32[1792]{0:T(1024)}, f32[1792]{0:T(1024)S(1)}, u32[]{:S(2)}) copy-start(f32[1792]{0:T(1024)S(1)} %get-tuple-element.543) | copy-start | bytes 21508
  92.3 41.6 %copy-start.40 = (f32[1792]{0:T(1024)}, f32[1792]{0:T(1024)S(1)}, u32[]{:S(2)}) copy-start(f32[1792]{0:T(1024)S(1)} %get-tuple-element.544) | copy-start | bytes 21508
  92.3 41.6 %copy-start.42 = (f32[1792]{0:T(1024)}, f32[1792]{0:T(1024)S(1)}, u32[]{:S(2)}) copy-start(f32[1792]{0:T(1024)S(1)} %get-tuple-element.545) | copy-start | bytes 21508
  92.3 41.6 %copy-start.44 = (f32[1792]{0:T(1024)}, f32[1792]{0:T(1024)S(1)}, u32[]{:S(2)}) copy-start(f32[1792]{0:T(1024)S(1)} %get-tuple-element.546) | copy-start | bytes 21508
  93.2 16.1 %copy-start.71 = (f32[24]{0:T(128)}, f32[24]{0:T(128)S(1)}, u32[]{:S(2)}) copy-start(f32[24]{0:T(128)S(1)} %get-tuple-element.691) | copy-start | bytes 292
  93.2 16.1 %copy-start.73 = (f32[24]{0:T(128)}, f32[24]{0:T(128)S(1)}, u32[]{:S(2)}) copy-start(f32[24]{0:T(128)S(1)} %get-tuple-element.692) | copy-start | bytes 292
  93.2 170.8 %copy-start.77 = (f32[24]{0:T(128)}, f32[24]{0:T(128)S(1)}, u32[]{:S(2)}) copy-start(f32[24]{0:T(128)S(1)} %get-tuple-element.690) | copy-start | bytes 292
  96.0 37.9 %copy-start.28 = (f32[1536]{0:T(1024)}, f32[1536]{0:T(1024)S(1)}, u32[]{:S(2)}) copy-start(f32[1536]{0:T(1024)S(1)} %get-tuple-element.671) | copy-start | bytes 18436
  96.0 37.9 %copy-start.30 = (f32[1536]{0:T(1024)}, f32[1536]{0:T(1024)S(1)}, u32[]{:S(2)}) copy-start(f32[1536]{0:T(1024)S(1)} %get-tuple-element.672) | copy-start | bytes 18436
  96.0 37.9 %copy-start.32 = (f32[1536]{0:T(1024)}, f32[1536]{0:T(1024)S(1)}, u32[]{:S(2)}) copy-start(f32[1536]{0:T(1024)S(1)} %get-tuple-element.673) | copy-start | bytes 18436
  96.0 37.9 %copy-start.34 = (f32[1536]{0:T(1024)}, f32[1536]{0:T(1024)S(1)}, u32[]{:S(2)}) copy-start(f32[1536]{0:T(1024)S(1)} %get-tuple-element.674) | copy-start | bytes 18436
  116.1 12.1 %collective-permute-start = (bf16[3,1792]{0,1:T(8,128)(2,1)}, bf16[3,1792]{0,1:T(8,128)(2,1)}, u32[]{:S(2)}, u32[]{:S(2)}) collective-permute-start(bf16[3,1792]{0,1:T(8,128)(2,1)} %slice.324), channel_id=1, source_target_pairs={{0,4},{4,8},{8,12},{12,16},{16,20},{20,24},{24,28},{1,5},{5,9},{9,... | collective-permute-start | bytes 32264 | tf_op jit(solution)/shard_map/ppermute | solution.py:28
  118.5 65.0 %copy-start.8 = (f32[6,24,2,128]{1,3,2,0:T(8,128)}, f32[6,24,2,128]{1,3,2,0:T(8,128)S(1)}, u32[]{:S(2)}) copy-start(f32[6,24,2,128]{1,3,2,0:T(8,128)S(1)} %copy.219) | copy-start | bytes 442372
  125.8 40.4 %copy-start.17 = (f32[6,256,24]{1,2,0:T(8,128)}, f32[6,256,24]{1,2,0:T(8,128)S(1)}, u32[]{:S(2)}) copy-start(f32[6,256,24]{1,2,0:T(8,128)S(1)} %copy.190) | copy-start | bytes 442372
  177.0 139.5 %all-gather.12.cloned.1.call-start = ((), (), s32[]{:S(2)}) async-start(), calls=%async_computation.4 | async-start | bytes 2433024 | tf_op jit(solution)/shard_map/all_gather | solution.py:187
  177.7 321.7 %all-gather.14.cloned.1.call-start = ((), (), s32[]{:S(2)}) async-start(), calls=%async_computation.5 | async-start | bytes 3538944 | tf_op jit(solution)/shard_map/all_gather | solution.py:34
  177.8 152.9 %copy-start.50 = (f32[12,128]{1,0:T(8,128)}, f32[12,128]{1,0:T(8,128)S(1)}, u32[]{:S(2)}) copy-start(f32[12,128]{1,0:T(8,128)S(1)} %slice_reduce_fusion.7) | copy-start | bytes 18436
  183.4 68.6 %copy-start.65 = (f32[24]{0:T(128)}, f32[24]{0:T(128)S(1)}, u32[]{:S(2)}) copy-start(f32[24]{0:T(128)S(1)} %get-tuple-element.680) | copy-start | bytes 292
  183.4 73.2 %copy-start.57 = (f32[24]{0:T(128)}, f32[24]{0:T(128)S(1)}, u32[]{:S(2)}) copy-start(f32[24]{0:T(128)S(1)} %get-tuple-element.678) | copy-start | bytes 292
  183.5 73.2 %copy-start.60 = (f32[24]{0:T(128)}, f32[24]{0:T(128)S(1)}, u32[]{:S(2)}) copy-start(f32[24]{0:T(128)S(1)} %get-tuple-element.679) | copy-start | bytes 292
  205.1 155.1 %copy-start.13 = (f32[6,256,24]{1,2,0:T(8,128)}, f32[6,256,24]{1,2,0:T(8,128)S(1)}, u32[]{:S(2)}) copy-start(f32[6,256,24]{1,2,0:T(8,128)S(1)} %copy.187) | copy-start | bytes 442372
  316.4 14.3 %copy-start.53 = (f32[1536]{0:T(1024)}, f32[1536]{0:T(1024)S(1)}, u32[]{:S(2)}) copy-start(f32[1536]{0:T(1024)S(1)} %fusion.135) | copy-start | bytes 18436
  368.9 389.0 %reduce-scatter.6.cloned.1.call-start = ((), (), s32[]{:S(2)}) async-start(), calls=%async_computation.6 | async-start | bytes 4866048 | tf_op jit(solution)/shard_map/reduce_scatter | solution.py:325
  373.7 91.3 %copy-start.14 = (f32[6,256,24]{1,2,0:T(8,128)S(1)}, f32[6,256,24]{1,2,0:T(8,128)}, u32[]{:S(2)}) copy-start(f32[6,256,24]{1,2,0:T(8,128)} %copy-done.13) | copy-start | bytes 442372
  465.0 20.5 %copy-start.27 = (f32[6,256,24]{1,2,0:T(8,128)S(1)}, f32[6,256,24]{1,2,0:T(8,128)}, u32[]{:S(2)}) copy-start(f32[6,256,24]{1,2,0:T(8,128)} %get-tuple-element.375) | copy-start | bytes 442372
  465.0 23.7 %copy-start.51 = (f32[12,128]{1,0:T(8,128)S(1)}, f32[12,128]{1,0:T(8,128)}, u32[]{:S(2)}) copy-start(f32[12,128]{1,0:T(8,128)} %copy-done.50) | copy-start | bytes 18436
  465.0 23.7 %copy-start.54 = (f32[1536]{0:T(1024)S(1)}, f32[1536]{0:T(1024)}, u32[]{:S(2)}) copy-start(f32[1536]{0:T(1024)} %copy-done.53) | copy-start | bytes 18436
  499.2 15.6 %copy-start.56 = (f32[24]{0:T(128)S(1)}, f32[24]{0:T(128)}, u32[]{:S(2)}) copy-start(f32[24]{0:T(128)} %get-tuple-element.675) | copy-start | bytes 292
  499.2 15.6 %copy-start.59 = (f32[24]{0:T(128)S(1)}, f32[24]{0:T(128)}, u32[]{:S(2)}) copy-start(f32[24]{0:T(128)} %copy-done.57) | copy-start | bytes 292
  499.3 15.6 %copy-start.62 = (f32[24]{0:T(128)S(1)}, f32[24]{0:T(128)}, u32[]{:S(2)}) copy-start(f32[24]{0:T(128)} %copy-done.60) | copy-start | bytes 292
  499.3 15.7 %copy-start.67 = (f32[24]{0:T(128)S(1)}, f32[24]{0:T(128)}, u32[]{:S(2)}) copy-start(f32[24]{0:T(128)} %copy-done.65) | copy-start | bytes 292
  499.3 330.8 %reduce-scatter.8.cloned.1.call-start = ((), (), s32[]{:S(2)}) async-start(), calls=%async_computation.7 | async-start | bytes 10948608
  521.5 16.3 %copy-start.5 = (f32[6,24,64,128]{3,2,1,0:T(8,128)}, f32[6,24,64,128]{3,2,1,0:T(8,128)S(1)}, u32[]{:S(2)}) copy-start(f32[6,24,64,128]{3,2,1,0:T(8,128)S(1)} %bitcast_dynamic-update-slice_fusion.4) | copy-start | bytes 14155780
  522.5 15.5 %copy-start.78 = (f32[24]{0:T(128)S(1)}, f32[24]{0:T(128)}, u32[]{:S(2)}) copy-start(f32[24]{0:T(128)} %copy-done.77) | copy-start | bytes 292
  576.7 17.5 %copy-start.39 = (f32[1792]{0:T(1024)S(1)}, f32[1792]{0:T(1024)}, u32[]{:S(2)}) copy-start(f32[1792]{0:T(1024)} %copy-done.38) | copy-start | bytes 21508
  576.7 17.5 %copy-start.41 = (f32[1792]{0:T(1024)S(1)}, f32[1792]{0:T(1024)}, u32[]{:S(2)}) copy-start(f32[1792]{0:T(1024)} %copy-done.40) | copy-start | bytes 21508
  576.7 17.5 %copy-start.43 = (f32[1792]{0:T(1024)S(1)}, f32[1792]{0:T(1024)}, u32[]{:S(2)}) copy-start(f32[1792]{0:T(1024)} %copy-done.42) | copy-start | bytes 21508
  576.7 17.5 %copy-start.45 = (f32[1792]{0:T(1024)S(1)}, f32[1792]{0:T(1024)}, u32[]{:S(2)}) copy-start(f32[1792]{0:T(1024)} %copy-done.44) | copy-start | bytes 21508
  594.2 18.5 %copy-start.9 = (f32[6,24,2,128]{1,3,2,0:T(8,128)S(1)}, f32[6,24,2,128]{1,3,2,0:T(8,128)}, u32[]{:S(2)}) copy-start(f32[6,24,2,128]{1,3,2,0:T(8,128)} %copy-done.8) | copy-start | bytes 442372
  594.2 18.5 %copy-start.12 = (f32[6,256,24]{2,1,0:T(8,128)S(1)}, f32[6,256,24]{2,1,0:T(8,128)}, u32[]{:S(2)}) copy-start(f32[6,256,24]{2,1,0:T(8,128)} %copy-done.11) | copy-start | bytes 442372
  594.2 18.5 %copy-start.15 = (f32[6,256,24]{2,1,0:T(8,128)S(1)}, f32[6,256,24]{2,1,0:T(8,128)}, u32[]{:S(2)}) copy-start(f32[6,256,24]{2,1,0:T(8,128)} %copy.203) | copy-start | bytes 442372
  594.2 18.5 %copy-start.16 = (f32[6,256,24]{2,1,0:T(8,128)S(1)}, f32[6,256,24]{2,1,0:T(8,128)}, u32[]{:S(2)}) copy-start(f32[6,256,24]{2,1,0:T(8,128)} %copy.207) | copy-start | bytes 442372
  594.2 18.5 %copy-start.47 = (f32[6,1,24]{2,0,1:T(8,128)S(1)}, f32[6,1,24]{2,0,1:T(8,128)}, u32[]{:S(2)}) copy-start(f32[6,1,24]{2,0,1:T(8,128)} %copy-done.46) | copy-start | bytes 1732
  635.9 23.6 %copy-start.72 = (f32[24]{0:T(128)S(1)}, f32[24]{0:T(128)}, u32[]{:S(2)}) copy-start(f32[24]{0:T(128)} %copy-done.71) | copy-start | bytes 292
  635.9 23.6 %copy-start.74 = (f32[24]{0:T(128)S(1)}, f32[24]{0:T(128)}, u32[]{:S(2)}) copy-start(f32[24]{0:T(128)} %copy-done.73) | copy-start | bytes 292
  635.9 24.8 %collective-permute-start.1 = (f32[3,1792]{1,0:T(4,128)S(1)}, f32[3,1792]{1,0:T(4,128)S(1)}, u32[]{:S(2)}, u32[]{:S(2)}) collective-permute-start(f32[3,1792]{1,0:T(4,128)S(1)} %copy.200), channel_id=1, source_target_pairs={{4,0},{8,4},{12,8},{16,12},{20,16},{24,20},{28,24},{5,1},{9,5},{13... | collective-permute-start | bytes 64520 | tf_op jit(solution)/shard_map/ppermute | solution.py:28
  698.4 15.9 %copy-start.69 = (f32[1536]{0:T(1024)S(1)}, f32[1536]{0:T(1024)}, u32[]{:S(2)}) copy-start(f32[1536]{0:T(1024)} %get-tuple-element.535) | copy-start | bytes 18436
  698.5 59.4 %copy-start.37 = (f32[1536]{0:T(1024)S(1)}, f32[1536]{0:T(1024)}, u32[]{:S(2)}) copy-start(f32[1536]{0:T(1024)} %copy-done.36) | copy-start | bytes 18436
  714.2 166.6 %copy-start.68 = (f32[4,56]{1,0:T(4,128)S(1)}, f32[4,56]{1,0:T(4,128)}, u32[]{:S(2)}) copy-start(f32[4,56]{1,0:T(4,128)} %param.37) | copy-start | bytes 2692
  714.2 166.6 %copy-start.79 = (f32[4,56]{1,0:T(4,128)S(1)}, f32[4,56]{1,0:T(4,128)}, u32[]{:S(2)}) copy-start(f32[4,56]{1,0:T(4,128)} %param.39) | copy-start | bytes 2692
  714.2 166.6 %copy-start.80 = (f32[4,56]{1,0:T(4,128)S(1)}, f32[4,56]{1,0:T(4,128)}, u32[]{:S(2)}) copy-start(f32[4,56]{1,0:T(4,128)} %param.38) | copy-start | bytes 2692
  714.2 168.0 %copy-start.85 = (f32[128]{0:T(128)S(1)}, f32[128]{0:T(128)}, u32[]{:S(2)}) copy-start(f32[128]{0:T(128)} %param.40) | copy-start | bytes 1540
  714.3 168.0 %copy-start.86 = (f32[128]{0:T(128)S(1)}, f32[128]{0:T(128)}, u32[]{:S(2)}) copy-start(f32[128]{0:T(128)} %param.42) | copy-start | bytes 1540
  714.3 168.0 %copy-start.87 = (f32[128]{0:T(128)S(1)}, f32[128]{0:T(128)}, u32[]{:S(2)}) copy-start(f32[128]{0:T(128)} %param.41) | copy-start | bytes 1540
  714.3 169.3 %copy-start.81 = (f32[3,24]{1,0:T(4,128)S(1)}, f32[3,24]{1,0:T(4,128)}, u32[]{:S(2)}) copy-start(f32[3,24]{1,0:T(4,128)} %param.45) | copy-start | bytes 868
  714.3 169.3 %copy-start.82 = (f32[3,24]{1,0:T(4,128)S(1)}, f32[3,24]{1,0:T(4,128)}, u32[]{:S(2)}) copy-start(f32[3,24]{1,0:T(4,128)} %param.44) | copy-start | bytes 868
  714.3 169.9 %copy-start.24 = (f32[48,768]{1,0:T(8,128)S(1)}, f32[48,768]{1,0:T(8,128)}, u32[]{:S(2)}) copy-start(f32[48,768]{1,0:T(8,128)} %param.34) | copy-start | bytes 442372
  714.3 169.9 %copy-start.26 = (f32[48,768]{1,0:T(8,128)S(1)}, f32[48,768]{1,0:T(8,128)}, u32[]{:S(2)}) copy-start(f32[48,768]{1,0:T(8,128)} %param.36) | copy-start | bytes 442372
  757.9 126.3 %copy-start.25 = (f32[48,768]{1,0:T(8,128)S(1)}, f32[48,768]{1,0:T(8,128)}, u32[]{:S(2)}) copy-start(f32[48,768]{1,0:T(8,128)} %reduce-scatter.6.cloned.1.call-done) | copy-start | bytes 442372
  834.3 51.6 %copy-start.21 = (f32[24,3352]{1,0:T(8,128)S(1)}, f32[24,3352]{1,0:T(8,128)}, u32[]{:S(2)}) copy-start(f32[24,3352]{1,0:T(8,128)} %param.31) | copy-start | bytes 965380
  834.4 51.6 %copy-start.22 = (f32[24,3352]{1,0:T(8,128)S(1)}, f32[24,3352]{1,0:T(8,128)}, u32[]{:S(2)}) copy-start(f32[24,3352]{1,0:T(8,128)} %reduce-scatter.8.cloned.1.call-done) | copy-start | bytes 965380
  (48 other events, 343.3 us)
Sparse Core Ops, SparseCore 0:
  11.5 68.7 all-gather.7
  177.1 60.8 all-gather.9
  241.5 55.8 all-gather.11
  369.0 58.5 all-gather.13
  499.4 105.0 reduce-scatter.5
  687.5 142.5 reduce-scatter.7
where the time goes:
time: 909 us; the launch traced here: 896 us
  other arithmetic  246 us (27%)
  matrix products  241 us (27%)
  blocking collectives  180 us (20%)
  local copies, waits for them, and re-layouts  126 us (14%)
  waiting for transfers between devices  73.2 us (8%)
  between operations  25.1 us (3%)
    unnamed x7, waiting for transfers between devices  70.7 us
    all_gather x1, blocking collectives, shards(): lax.all_gather(vectors.astype(jnp.bfloat16), ('seq', 'rep'), axis=0, tile...  43.1 us
    unnamed x1, blocking collectives  42.1 us
    another operation x12, other arithmetic  40.5 us
    psum x1, blocking collectives, shards(): total_sq, head_sum = lax.psum((owned_sq, head_grad_local), ('seq', 'rep'))  39.6 us
    all_gather x1, blocking collectives, shards(): lax.all_gather(conv_weight.astype(jnp.bfloat16), ('seq', 'rep'), axis=1,...  36.7 us
    reduce_sum x6, other arithmetic, intra_backward(): grad_cumul = (jnp.sum(flow, axis=2) - jnp.sum(flow, axis=1)).T  26.3 us
    unnamed x213, local copies, waits for them, and re-layouts  25.6 us
  transfers between devices with their start and end apart: 8, of which 2 were waited for; matrix products, arithmetic and copies ran while one was open for 53% of the time, Pallas kernels for 0%

commit v1 on v0

v1 whole, which is shorter than its diff:
```python
from functools import partial

import jax
import jax.numpy as jnp
from jax import lax
from jax.experimental import pallas as pl
from jax.experimental.pallas import tpu as pltpu
from jax.sharding import PartitionSpec as P

SPAN = 256
HALF = 128
LANES = 128
STRIP = 256
TILE = 64
STEP = 10

EPS_NORM = 1e-05
MAX_NORM = 1.0
BETA_ONE = 0.9
BETA_TWO = 0.95
ADAM_EPS = 1e-08
DECAY_MAT = 0.1
RATE_MAT = 0.05
RATE_CONV = 0.5
RATE_VEC = 1.0
RATE_HEAD = 2.0
VMEM_BYTES = 56 * 1024 * 1024

f32 = jnp.float32
bf16 = jnp.bfloat16


def dot(a, b):
    return jnp.dot(a, b, preferred_element_type=f32)


def dot_nt(a, b):
    return lax.dot_general(a, b, (((1,), (1,)), ((), ())), preferred_element_type=f32)


def dot_tn(a, b):
    return lax.dot_general(a, b, (((0,), (0,)), ((), ())), preferred_element_type=f32)


def two_terms(v):
    high = v.astype(bf16)
    return high, (v - high.astype(f32)).astype(bf16)


def split_lanes(v):
    return jnp.concatenate(two_terms(v), axis=-1)


def exact_dot(ones_matrix, v):
    high, rest = two_terms(v)
    middle, low = two_terms(v - high.astype(f32))
    return dot(ones_matrix, high) + (dot(ones_matrix, middle) + dot(ones_matrix, low))


def head_sums(v, reducer):
    high, low = two_terms(v)
    return dot(high, reducer) + dot(low, reducer)


def sigmoid(v):
    return 0.5 * jnp.tanh(0.5 * v) + 0.5


def block_diag(pair):
    low_lanes = lax.broadcasted_iota(jnp.int32, pair.shape, 1) < LANES // 2
    none = jnp.zeros_like(pair)
    return jnp.concatenate(
        [jnp.where(low_lanes, pair, none), jnp.where(low_lanes, none, pair)], axis=0
    )


def eight_rows(v):
    return jnp.sum(v.reshape(v.shape[0] // 8, 8, v.shape[1]), axis=0)


def row_norm(rows, gain):
    wide = rows.astype(f32)
    factor = lax.rsqrt(jnp.mean(wide * wide, axis=-1, keepdims=True) + EPS_NORM)
    return (wide * factor * gain).astype(bf16)


def front_kernel(
    u_ref, before_ref, meta_ref, w_ref, gain_ref, taps_ref, bias_ref, heads_ref, ex_ref, tri_ref,
    normed_ref, conv_ref, act_ref, slope_ref, dt_ref, cum_ref, cumdev_ref, raw_ref, inc_ref,
    rim_ref, state_out_ref, total_ref,
    ext, state, offset,
    *, conv_dim, inner, places,
):
    step = pl.program_id(0)
    gain = gain_ref[...]
    keep = meta_ref[0:1, 3:4]

    @pl.when(step == 0)
    def _():
        rim = dot(row_norm(before_ref[...], gain), w_ref[:, :conv_dim]).astype(bf16)
        rim_ref[...] = rim
        ext[0:8, :] = rim[8:16].astype(f32) * keep
        state[...] = jnp.zeros_like(state)
        offset[...] = jnp.zeros_like(offset)

    @pl.when(step > 0)
    def _():
        ext[0:8, :] = ext[SPAN : SPAN + 8, :] * keep

    normed_ref[...] = row_norm(u_ref[...], gain)
    for s in range(0, conv_dim, STRIP):
        cols = slice(s, s + STRIP)
        piece = dot(normed_ref[...], w_ref[:, cols]).astype(bf16)
        conv_ref[:, cols] = piece
        ext[8 : 8 + SPAN, cols] = piece.astype(f32)
    raw = dot(normed_ref[...], w_ref[:, conv_dim : conv_dim + LANES]).astype(bf16).astype(f32)
    raw = raw + heads_ref[0:1, :]
    raw_ref[...] = raw
    dt_values = meta_ref[:, 0:1] * (jnp.maximum(raw, 0.0) + jnp.log1p(jnp.exp(-jnp.abs(raw))))
    dt_ref[...] = dt_values
    for s in range(0, conv_dim, STRIP):
        cols = slice(s, s + STRIP)
        for base in range(0, SPAN, TILE):
            total = bias_ref[0:1, cols]
            for k in range(4):
                total = total + taps_ref[k : k + 1, cols] * ext[base + 5 + k : base + 5 + k + TILE, cols]
            gate = sigmoid(total)
            value = total * gate
            act_ref[base : base + TILE, cols] = value.astype(bf16)
            slope_ref[base : base + TILE, cols] = (gate + value * (1.0 - gate)).astype(bf16)
    for c in range(SPAN // HALF):
        rows = slice(c * HALF, (c + 1) * HALF)
        dt_here = dt_values[rows]
        cumul = exact_dot(tri_ref[...], heads_ref[1:2, :] * dt_here)
        cum_ref[rows, :] = cumul
        cumdev_ref[rows, :] = offset[0:1, :] + cumul
        last = cumul[HALF - 1 : HALF]
        offset[...] = offset[...] + last
        keep_here = meta_ref[c * HALF : c * HALF + 1, 3:4]
        weights = split_lanes(jnp.exp(last - cumul) * dt_here)
        fade = split_lanes(jnp.broadcast_to(jnp.exp(last), (8, LANES)))
        b_rows = act_ref[rows, inner : inner + LANES]
        for s in range(0, inner, STRIP):
            cols = slice(s, s + STRIP)
            scaled = (act_ref[rows, cols].astype(f32) * dot(weights, ex_ref[:, cols])).astype(bf16)
            arrived = keep_here * state[:, cols]
            inc_ref[rows, cols] = arrived.astype(bf16)
            state[:, cols] = dot(fade, ex_ref[:, cols])[0:1] * arrived + dot_tn(b_rows, scaled)

    @pl.when(step == pl.num_programs(0) - 1)
    def _():
        state_out_ref[:, :inner] = state[...].astype(bf16)
        gain_row = jnp.exp(offset[0:1, :]) * meta_ref[SPAN - 1 : SPAN, 1:2]
        high, low = two_terms(jnp.broadcast_to(gain_row, (HALF, LANES)))
        place = lax.broadcasted_iota(jnp.int32, (HALF, LANES), 0) % (HALF // places)
        none = jnp.zeros_like(high)
        state_out_ref[:, inner:] = jnp.where(
            place == 0, high, jnp.where(place == 1, low, none)
        )
        total_ref[...] = offset[...]


def chain_kernel(states_ref, gains_ref, ex_ref, out_ref, *, reverse):
    places, rows, inner = out_ref.shape
    gains = jnp.concatenate([gains_ref[:, 0, :], gains_ref[:, 1, :]], axis=1)
    wide = dot(gains, ex_ref[...])
    running = jnp.zeros((rows, inner), f32)
    for k in range(places):
        at = places - 1 - k if reverse else k
        out_ref[at] = running.astype(bf16)
        running = wide[at : at + 1] * running + states_ref[at, :, :inner].astype(f32)


def intra_kernel(
    act_ref, dt_ref, cum_ref, inc_ref, normed_ref, w_ref, ex_ref, y_ref, gate_ref, *, inner
):
    for s in range(0, inner, STRIP):
        cols = slice(s, s + STRIP)
        gate_ref[:, cols] = dot(normed_ref[...], w_ref[:, cols]).astype(bf16)
    at_row = lax.broadcasted_iota(jnp.int32, (HALF, HALF), 0)
    at_col = lax.broadcasted_iota(jnp.int32, (HALF, HALF), 1)
    for c in range(SPAN // HALF):
        rows = slice(c * HALF, (c + 1) * HALF)
        b_rows = act_ref[rows, inner : inner + LANES]
        c_rows = act_ref[rows, inner + LANES : inner + 2 * LANES]
        scores = jnp.where(at_row >= at_col, dot_nt(c_rows, b_rows), 0.0)
        cumul = cum_ref[rows, :]
        across = cumul.T
        dt_split = split_lanes(dt_ref[rows, :])
        grown = split_lanes(jnp.exp(cumul))
        for s in range(0, inner, STRIP):
            cols = slice(s, s + STRIP)
            steps = (act_ref[rows, cols].astype(f32) * dot(dt_split, ex_ref[:, cols])).astype(bf16)
            inter = dot(c_rows, inc_ref[rows, cols]) * dot(grown, ex_ref[:, cols])
            for q in range(STRIP // LANES):
                mixes = []
                for h in (s // 64 + 2 * q, s // 64 + 2 * q + 1):
                    fall = jnp.minimum(cumul[:, h : h + 1] - across[h : h + 1, :], 0.0)
                    mixes.append((scores * jnp.exp(fall)).astype(bf16))
                lanes = slice(q * LANES, (q + 1) * LANES)
                y_ref[rows, s + q * LANES : s + (q + 1) * LANES] = (
                    dot(jnp.concatenate(mixes, axis=1), block_diag(steps[:, lanes]))
                    + inter[:, lanes]
                )


def gate_kernel(
    y_ref, act_ref, prefix_ref, cumdev_ref, meta_ref, gate_ref, w_ref, cot_ref, skip_ref, gain_ref,
    ex_ref, red_ref,
    low_ref, gm_ref, dgate_ref, back_ref, r_ref, gdev_ref, sums_ref,
    y_all, g_all, d_all, e_all, gdev,
    *, inner,
):
    step = pl.program_id(0)

    @pl.when(step == 0)
    def _():
        gdev[...] = jnp.zeros_like(gdev)
        sums_ref[...] = jnp.zeros_like(sums_ref)

    c_rows = act_ref[:, inner + LANES : inner + 2 * LANES]
    reach = split_lanes(jnp.exp(cumdev_ref[...]) * meta_ref[:, 1:2])
    back = (meta_ref[:, 0:1] * cot_ref[...].astype(f32)).astype(bf16)
    back_ref[...] = back
    tiles = [slice(base, base + TILE) for base in range(0, SPAN, TILE)]
    squares = [jnp.zeros((TILE, 1), f32) for _ in tiles]
    for s in range(0, inner, STRIP):
        cols = slice(s, s + STRIP)
        e_all[:, cols] = dot(reach, ex_ref[:, cols])
        y_all[:, cols] = dot(c_rows, prefix_ref[:, cols])
        d_all[:, cols] = dot_nt(back, w_ref[cols, :])
        for at, rows in enumerate(tiles):
            y = y_ref[rows, cols] + e_all[rows, cols] * y_all[rows, cols]
            y_all[rows, cols] = y
            z = gate_ref[rows, cols].astype(f32)
            mixed = y + skip_ref[0:1, cols] * act_ref[rows, cols].astype(f32)
            g = mixed * (z * sigmoid(z))
            g_all[rows, cols] = g
            squares[at] = squares[at] + jnp.sum(g * g, axis=1, keepdims=True)
    factors = [lax.rsqrt(v / inner + EPS_NORM) for v in squares]
    inner_sums = [jnp.zeros((TILE, 1), f32) for _ in tiles]
    for s in range(0, inner, STRIP):
        cols = slice(s, s + STRIP)
        gain = gain_ref[0:1, cols]
        gain_sum = jnp.zeros((8, STRIP), f32)
        for at, rows in enumerate(tiles):
            gn = g_all[rows, cols] * factors[at]
            g_all[rows, cols] = gn
            low_ref[rows, cols] = (gn * gain).astype(bf16)
            raw = d_all[rows, cols]
            gain_sum = gain_sum + eight_rows(raw * gn)
            d = raw * gain
            d_all[rows, cols] = d
            inner_sums[at] = inner_sums[at] + jnp.sum(d * gn, axis=1, keepdims=True)
        sums_ref[0:8, cols] = sums_ref[0:8, cols] + gain_sum
    means = [v / inner for v in inner_sums]
    r_parts = [jnp.zeros((TILE, LANES), f32) for _ in tiles]
    for s in range(0, inner, STRIP):
        cols = slice(s, s + STRIP)
        skip_sum = jnp.zeros((8, STRIP), f32)
        for at, rows in enumerate(tiles):
            dg = factors[at] * (d_all[rows, cols] - g_all[rows, cols] * means[at])
            z = gate_ref[rows, cols].astype(f32)
            sg = sigmoid(z)
            sl = z * sg
            x = act_ref[rows, cols].astype(f32)
            y = y_all[rows, cols]
            mixed = y + skip_ref[0:1, cols] * x
            gm_low = (dg * sl).astype(bf16)
            gm_ref[rows, cols] = gm_low
            dgate_ref[rows, cols] = (dg * mixed * (sg + sl * (1.0 - sg))).astype(bf16)
            gm = gm_low.astype(f32)
            skip_sum = skip_sum + eight_rows(gm * x)
            r_parts[at] = r_parts[at] + head_sums(gm * y, red_ref[cols, :])
            e_all[rows, cols] = gm * e_all[rows, cols]
        sums_ref[8:16, cols] = sums_ref[8:16, cols] + skip_sum
        gdev[:, cols] = gdev[:, cols] + dot_tn(c_rows, e_all[:, cols].astype(bf16))
    for at, rows in enumerate(tiles):
        r_ref[rows, :] = r_parts[at]

    @pl.when(step == pl.num_programs(0) - 1)
    def _():
        gdev_ref[...] = gdev[...].astype(bf16)


def intra_back_kernel(
    act_ref, gm_ref, dt_ref, cum_ref, cumdev_ref, meta_ref, inc_ref, prefix_ref, r_ref, ex_ref,
    red_ref, tri_up_ref,
    dx_ref, dbc_ref, xd_ref, da_ref,
    de, dlast,
    *, inner,
):
    @pl.when(pl.program_id(0) == 0)
    def _():
        de[...] = jnp.zeros_like(de)
        dlast[...] = jnp.zeros_like(dlast)

    at_row = lax.broadcasted_iota(jnp.int32, (HALF, HALF), 0)
    at_col = lax.broadcasted_iota(jnp.int32, (HALF, HALF), 1)
    upper = at_row <= at_col
    for c in reversed(range(SPAN // HALF)):
        rows = slice(c * HALF, (c + 1) * HALF)
        first = slice(c * HALF, c * HALF + 1)
        b_rows = act_ref[rows, inner : inner + LANES]
        c_rows = act_ref[rows, inner + LANES : inner + 2 * LANES]
        scores = jnp.where(upper, dot_nt(b_rows, c_rows), 0.0)
        cumul = cum_ref[rows, :]
        across = cumul.T
        last = cumul[HALF - 1 : HALF]
        dt_split = split_lanes(dt_ref[rows, :])
        grown = split_lanes(jnp.exp(cumul))
        left = split_lanes(jnp.exp(last - cumul))
        fade = split_lanes(jnp.broadcast_to(jnp.exp(last), (8, LANES)))
        start = jnp.exp(cumdev_ref[first, :] - cum_ref[first, :]) * meta_ref[first, 1:2]
        start = split_lanes(jnp.broadcast_to(start, (8, LANES)))
        keep = meta_ref[first, 3:4]
        d_scores = jnp.zeros((HALF, HALF), f32)
        d_c = jnp.zeros((HALF, LANES), f32)
        d_b = jnp.zeros((HALF, LANES), f32)
        x_dot = jnp.zeros((HALF, LANES), f32)
        d_end = jnp.zeros((8, LANES), f32)
        for s in range(0, inner, STRIP):
            cols = slice(s, s + STRIP)
            x = act_ref[rows, cols].astype(f32)
            left_wide = dot(left, ex_ref[:, cols])
            steps = (x * dot(dt_split, ex_ref[:, cols])).astype(bf16)
            gm = gm_ref[rows, cols]
            gm_grown = (gm.astype(f32) * dot(grown, ex_ref[:, cols])).astype(bf16)
            start_wide = dot(start, ex_ref[:, cols])[0:1]
            arrived = inc_ref[rows, cols].astype(f32) + start_wide * prefix_ref[:, cols].astype(f32)
            d_c = d_c + dot_nt(gm_grown, arrived.astype(bf16))
            de_here = de[:, cols]
            de_low = de_here.astype(bf16)
            dx_far = left_wide * dot(b_rows, de_low)
            d_b = d_b + dot_nt((steps.astype(f32) * left_wide).astype(bf16), de_low)
            for q in range(STRIP // LANES):
                lanes = slice(q * LANES, (q + 1) * LANES)
                gm_diag = block_diag(gm[:, lanes])
                d_mix = dot_nt(steps[:, lanes], gm_diag)
                mixes = []
                for k in range(2):
                    h = s // 64 + 2 * q + k
                    decay = jnp.exp(jnp.minimum(across[h : h + 1, :] - cumul[:, h : h + 1], 0.0))
                    mixes.append((scores * decay).astype(bf16))
                    d_scores = d_scores + d_mix[:, k * HALF : (k + 1) * HALF] * decay
                dx = dot(jnp.concatenate(mixes, axis=1), gm_diag) + dx_far[:, lanes]
                wide = slice(s + q * LANES, s + (q + 1) * LANES)
                dx_ref[rows, wide] = dx.astype(bf16)
                x_dot = x_dot + head_sums(x[:, lanes] * dx, red_ref[wide, :])
            de_new = keep * (
                dot_tn(c_rows, gm_grown) + dot(fade, ex_ref[:, cols])[0:1] * de_here
            )
            de[:, cols] = de_new
            d_end = d_end + head_sums(eight_rows(de_new * arrived), red_ref[cols, :])
        xd_ref[rows, :] = x_dot
        da_ref[rows, :] = (
            exact_dot(tri_up_ref[...], r_ref[rows, :] - dt_ref[rows, :] * x_dot) + dlast[0:1, :]
        )
        dlast[...] = jnp.broadcast_to(jnp.sum(d_end, axis=0, keepdims=True), dlast.shape)
        d_low = jnp.where(upper, d_scores, 0.0).astype(bf16)
        dbc_ref[rows, :LANES] = dot(d_low, c_rows) + d_b
        dbc_ref[rows, LANES:] = dot_tn(d_low, b_rows) + d_c


def outer_kernel(
    u_ref, meta_ref, low_ref, back_ref, normed_ref, dgate_ref, w_ref,
    out_ref, out_grad_ref, gate_grad_ref,
    out_sum, gate_sum,
):
    step = pl.program_id(0)

    @pl.when(step == 0)
    def _():
        out_sum[...] = jnp.zeros_like(out_sum)
        gate_sum[...] = jnp.zeros_like(gate_sum)

    branch = dot(low_ref[...], w_ref[...])
    out_ref[...] = (u_ref[...].astype(f32) + meta_ref[:, 0:1] * branch).astype(bf16)
    out_sum[...] = out_sum[...] + dot_tn(low_ref[...], back_ref[...])
    gate_sum[...] = gate_sum[...] + dot_tn(normed_ref[...], dgate_ref[...])

    @pl.when(step == pl.num_programs(0) - 1)
    def _():
        out_grad_ref[...] = out_sum[...].astype(bf16)
        gate_grad_ref[...] = gate_sum[...].astype(bf16)


def conv_back_kernel(
    act_ref, slope_ref, conv_ref, dx_ref, gm_ref, dbc_ref, dt_ref, cumdev_ref, raw_ref, xd_ref,
    da_ref, meta_ref, above_ref, prefix_ref, total_ref, pre_ref, skip_ref, taps_ref, heads_ref, rim_ref,
    ex_ref, red_ref, tri_ref,
    dconv_ref, first_ref, sums_ref, hsums_ref,
    fresh, kept, ext, dt_fresh, dt_kept, flow,
    *, inner, conv_dim, num_heads,
):
    step = pl.program_id(0)
    blocks = pl.num_programs(0) - 1
    keep = meta_ref[0:1, 3:4]

    @pl.when(step == 0)
    def _():
        ext[0:8, :] = rim_ref[8:16, :].astype(f32) * keep
        sums_ref[...] = jnp.zeros_like(sums_ref)
        hsums_ref[...] = jnp.zeros_like(hsums_ref)
        start = jnp.zeros((8, LANES), f32)
        for s in range(0, inner, STRIP):
            cols = slice(s, s + STRIP)
            both = above_ref[:, cols].astype(f32) * prefix_ref[:, cols].astype(f32)
            start = start + head_sums(eight_rows(both), red_ref[cols, :])
        start = jnp.sum(start, axis=0, keepdims=True)
        flow[...] = start * jnp.exp(total_ref[...]) * pre_ref[...]

    @pl.when((step > 0) & (step < blocks))
    def _():
        ext[0:8, :] = ext[SPAN : SPAN + 8, :] * keep

    @pl.when(step < blocks)
    def _():
        ext[8 : 8 + SPAN, :] = conv_ref[...].astype(f32)
        for c in range(SPAN // HALF):
            rows = slice(c * HALF, (c + 1) * HALF)
            b_rows = act_ref[rows, inner : inner + LANES]
            dt_here = dt_ref[rows, :]
            ahead = split_lanes(jnp.exp(total_ref[0:1, :] - cumdev_ref[rows, :]) * meta_ref[rows, 2:3])
            dt_split = split_lanes(dt_here)
            x_dot = jnp.zeros((HALF, LANES), f32)
            d_b = dbc_ref[rows, :LANES]
            for s in range(0, inner, STRIP):
                cols = slice(s, s + STRIP)
                x = act_ref[rows, cols].astype(f32)
                dt_wide = dot(dt_split, ex_ref[:, cols])
                ahead_wide = dot(ahead, ex_ref[:, cols])
                far = ahead_wide * dot(b_rows, above_ref[:, cols])
                dx = dt_wide * (dx_ref[rows, cols].astype(f32) + far)
                dx = dx + skip_ref[0:1, cols] * gm_ref[rows, cols].astype(f32)
                fresh[rows, cols] = dx * slope_ref[rows, cols].astype(f32)
                x_dot = x_dot + head_sums(x * far, red_ref[cols, :])
                d_b = d_b + dot_nt((x * dt_wide * ahead_wide).astype(bf16), above_ref[:, cols])
            b_cols = slice(inner, inner + LANES)
            c_cols = slice(inner + LANES, inner + 2 * LANES)
            fresh[rows, b_cols] = d_b * slope_ref[rows, b_cols].astype(f32)
            fresh[rows, c_cols] = dbc_ref[rows, LANES:] * slope_ref[rows, c_cols].astype(f32)
            passed = dt_here * x_dot
            da = da_ref[rows, :] + flow[0:1, :] + exact_dot(tri_ref[...], passed) - passed
            flow[...] = flow[...] + jnp.sum(passed, axis=0, keepdims=True)
            rate = heads_ref[1:2, :]
            hsums_ref[8:16, :] = hsums_ref[8:16, :] + eight_rows(da * rate * dt_here)
            d_dt = xd_ref[rows, :] + x_dot + rate * da
            d_raw = meta_ref[rows, 0:1] * sigmoid(raw_ref[rows, :]) * d_dt
            real = lax.broadcasted_iota(jnp.int32, d_raw.shape, 1) < num_heads
            d_raw = jnp.where(real, d_raw, 0.0)
            hsums_ref[0:8, :] = hsums_ref[0:8, :] + eight_rows(d_raw)
            dt_fresh[rows, :] = d_raw.astype(bf16)
        for s in range(0, conv_dim, STRIP):
            cols = slice(s, s + STRIP)
            sums = [jnp.zeros((8, STRIP), f32) for _ in range(5)]
            for base in range(0, SPAN, TILE):
                d = fresh[base : base + TILE, cols]
                sums[4] = sums[4] + eight_rows(d)
                for k in range(4):
                    sums[k] = sums[k] + eight_rows(d * ext[base + 5 + k : base + 5 + k + TILE, cols])
            for k in range(5):
                at = slice(8 * k, 8 * k + 8)
                sums_ref[at, cols] = sums_ref[at, cols] + sums[k]

    @pl.when(step == 0)
    def _():
        first_ref[...] = fresh[0:8, :] * keep

    @pl.when(step > 0)
    def _():
        inside = (step < blocks).astype(f32)
        kept[SPAN : SPAN + 8, :] = fresh[0:8, :] * (keep * inside)
        for s in range(0, conv_dim, STRIP):
            cols = slice(s, s + STRIP)
            for base in range(0, SPAN, TILE):
                total = taps_ref[3:4, cols] * kept[base : base + TILE, cols]
                for k in range(3):
                    total = total + taps_ref[k : k + 1, cols] * kept[base + 3 - k : base + 3 - k + TILE, cols]
                dconv_ref[base : base + TILE, cols] = total.astype(bf16)
        dconv_ref[:, conv_dim:] = dt_kept[...]

    kept[0:SPAN, :] = fresh[...]
    dt_kept[...] = dt_fresh[...]


def weight_grad_kernel(normed_ref, dconv_ref, small_ref, out_ref, total, *, conv_dim):
    step = pl.program_id(0)

    @pl.when(step == 0)
    def _():
        total[...] = jnp.zeros_like(total)

    total[...] = total[...] + dot_tn(normed_ref[...], dconv_ref[...])

    @pl.when(step == pl.num_programs(0) - 1)
    def _():
        width = total.shape[1]
        out_ref[:, :conv_dim] = total[:, :conv_dim].astype(bf16)
        out_ref[:, conv_dim:] = (total[:, conv_dim:] + small_ref[...]).astype(bf16)


def input_grad_kernel(
    dconv_ref, dgate_ref, wc_ref, wg_ref, u_ref, cot_ref, gain_ref, out_ref, sums_ref
):
    @pl.when(pl.program_id(0) == 0)
    def _():
        sums_ref[...] = jnp.zeros_like(sums_ref)

    grad = dot_nt(dconv_ref[...], wc_ref[...]) + dot_nt(dgate_ref[...], wg_ref[...])
    wide = u_ref[...].astype(f32)
    factor = lax.rsqrt(jnp.mean(wide * wide, axis=-1, keepdims=True) + EPS_NORM)
    unit = wide * factor
    sums_ref[...] = sums_ref[...] + eight_rows(grad * unit)
    d = grad * gain_ref[...]
    du = factor * (d - unit * jnp.mean(d * unit, axis=-1, keepdims=True))
    out_ref[...] = (cot_ref[...].astype(f32) + du).astype(bf16)


def adam_step(master, clipped, first_m, second_m, step_rate, decay_rate):
    first_new = BETA_ONE * first_m + (1.0 - BETA_ONE) * clipped
    second_new = BETA_TWO * second_m + (1.0 - BETA_TWO) * clipped * clipped
    first_hat = first_new / (1.0 - BETA_ONE**STEP)
    second_hat = second_new / (1.0 - BETA_TWO**STEP)
    master_new = master - step_rate * (
        first_hat / (jnp.sqrt(second_hat) + ADAM_EPS) + decay_rate * master
    )
    return (first_new, second_new, master_new, master_new.astype(jnp.bfloat16))


def shift(value, axis, steps):
    count = lax.axis_size(axis)
    initial, last = (max(0, -steps), min(count, count - steps))
    return lax.ppermute(value, axis, [(source, source + steps) for source in range(initial, last)])


def axis_bits(axis):
    return [(axis, 1 << k) for k in reversed(range(lax.axis_size(axis).bit_length() - 1))]


def swap(value, axis, bit):
    count = lax.axis_size(axis)
    return lax.ppermute(value, axis, [(k, k ^ bit) for k in range(count)])


def my_bit(axis, bit):
    return (lax.axis_index(axis) // bit) % 2


def gather_rows(shard):
    bits = axis_bits("seq") + axis_bits("rep")
    value = shard
    known = []
    for axis, bit in bits:
        other = swap(value, axis, bit)
        mine = my_bit(axis, bit)
        place = len(known)
        pair = jnp.where(
            mine == 0,
            jnp.stack([value, other], axis=place),
            jnp.stack([other, value], axis=place),
        )
        value = pair
        known.append((axis, bit))
    return value.reshape((-1,) + shard.shape[1:])


def scatter_sum(whole):
    bits = axis_bits("seq") + axis_bits("rep")
    count = lax.axis_size("seq") * lax.axis_size("rep")
    value = whole.reshape((2,) * len(bits) + (whole.shape[0] // count,) + whole.shape[1:])
    for axis, bit in reversed(bits):
        place = bits.index((axis, bit))
        mine = my_bit(axis, bit)
        given = lax.dynamic_index_in_dim(value, 1 - mine, place, keepdims=False)
        held = lax.dynamic_index_in_dim(value, mine, place, keepdims=False)
        got = swap(given, axis, bit)
        value = (held.astype(f32) + got.astype(f32)).astype(bf16)
        bits = bits[:place] + bits[place + 1 :]
    return value.astype(f32)


def call(kernel, grid, ins, in_blocks, outs, out_blocks, scratch, flops, **fixed):
    moved = sum(v.size * v.dtype.itemsize for v in ins) + sum(v.size * v.dtype.itemsize for v in outs)
    return pl.pallas_call(
        partial(kernel, **fixed),
        grid=(grid,),
        in_specs=in_blocks,
        out_specs=out_blocks,
        out_shape=outs,
        scratch_shapes=scratch,
        compiler_params=pltpu.CompilerParams(
            dimension_semantics=("arbitrary",), vmem_limit_bytes=VMEM_BYTES
        ),
        cost_estimate=pl.CostEstimate(flops=int(flops), bytes_accessed=moved, transcendentals=0),
    )(*ins)


def full(shape):
    return pl.BlockSpec(shape, lambda i: (0,) * len(shape))


def rows_of(count, width, index=lambda i: i):
    return pl.BlockSpec((count, width), lambda i: (index(i), 0))


def like(*shape, dtype=f32):
    return jax.ShapeDtypeStruct(shape, dtype)


def seq_meta(lengths, offset, row_count):
    blocks = (lengths + SPAN - 1) // SPAN
    seq_ends = SPAN * jnp.cumsum(blocks)
    begins = seq_ends - SPAN * blocks
    position = offset + jnp.arange(row_count, dtype=jnp.int32)
    is_after = position[:, None] >= begins[None, :]
    inside = is_after & (position[:, None] < (begins + lengths)[None, :])
    live = jnp.any(inside, axis=1)
    first = jnp.max(jnp.where(is_after, begins[None, :], 0), axis=1)
    chunk_start = position - position % HALF
    flags = [live, first < offset, first == first[-1], first < chunk_start]
    return jnp.stack([flag.astype(f32) for flag in flags] + [jnp.zeros_like(position, f32)] * 4, axis=1)


def shards(
    tokens,
    cotangent,
    seq_lengths,
    in_weight,
    in_first,
    in_second,
    out_weight,
    out_first,
    out_second,
    conv_weight,
    conv_first,
    conv_second,
    vectors,
    vec_first,
    vec_second,
    head_params,
    head_first,
    head_second,
):
    u = tokens[0]
    cot = cotangent[0]
    rows, model = u.shape
    ranks = lax.axis_size("seq") * lax.axis_size("rep")
    places = lax.axis_size("seq")
    own_rows = in_weight.shape[0]
    taps_own = conv_weight.shape[1]
    vecs_own = vectors.shape[0]
    conv_dim = taps_own * ranks
    inner = out_weight.shape[0] * ranks
    heads = head_params.shape[1]
    head_dim = inner // heads
    nblk = rows // SPAN
    spare = LANES - heads
    smalls = 4 * taps_own + vecs_own

    meta = seq_meta(seq_lengths[0], lax.axis_index("seq") * rows, rows)
    before = shift(u[rows - 16 :], "seq", 1)

    in_low = in_weight.astype(bf16)
    packed = jnp.concatenate([conv_weight.reshape(-1), vectors]).astype(bf16)
    packed = jnp.pad(packed, (0, own_rows * spare - smalls)).reshape(own_rows, spare)
    conv_shard = jnp.concatenate([in_low[:, inner:], packed], axis=1)
    w_conv = gather_rows(conv_shard)
    w_gate = lax.all_gather(in_low[:, :inner], ("seq", "rep"), axis=0, tiled=True)
    w_out = lax.all_gather(out_weight.astype(bf16), ("seq", "rep"), axis=0, tiled=True)

    small = w_conv[:, conv_dim + heads :].reshape(ranks, own_rows * spare).astype(f32)
    taps = small[:, : 4 * taps_own].reshape(ranks, 4, taps_own).transpose(1, 0, 2).reshape(4, conv_dim)
    vecs = small[:, 4 * taps_own : smalls].reshape(-1)
    norm_gain = vecs[None, :model]
    gate_gain = vecs[None, model : model + inner]
    conv_bias = vecs[None, model + inner :]
    head_rows = jnp.stack([head_params[0], -jnp.exp(head_params[1]), head_params[2]])
    head_rows = jnp.pad(head_rows, ((0, 5), (0, spare)))
    skip_wide = jnp.repeat(head_params[2], head_dim)[None]

    lane_head = jnp.arange(inner, dtype=jnp.int32) // head_dim
    spread = (jnp.arange(LANES, dtype=jnp.int32)[:, None] == lane_head[None]).astype(bf16)
    ex = jnp.concatenate([spread, spread], axis=0)
    red = (lane_head[:, None] == jnp.arange(LANES, dtype=jnp.int32)[None]).astype(bf16)
    order = jnp.arange(HALF, dtype=jnp.int32)
    tri = (order[:, None] >= order[None]).astype(bf16)
    tri_up = (order[:, None] <= order[None]).astype(bf16)

    wide = conv_dim + LANES
    b_act = rows_of(SPAN, conv_dim)
    b_in = rows_of(SPAN, inner)
    b_lane = rows_of(SPAN, LANES)
    b_model = rows_of(SPAN, model)
    b_meta = rows_of(SPAN, 8)
    b_ex = full((2 * LANES, inner))
    b_red = full((inner, LANES))
    b_tri = full((HALF, HALF))
    b_heads = full((8, LANES))
    lane_out = like(rows, LANES)

    (
        normed, conv_in, act, slope, dt_values, cumul, cumdev, raw, own_inc, rim, state_out, total
    ) = call(
        front_kernel,
        nblk,
        [u, before, meta, w_conv, norm_gain, taps, conv_bias, head_rows, ex, tri],
        [
            b_model, full((16, model)), b_meta, full((model, wide)), full((1, model)),
            full((4, conv_dim)), full((1, conv_dim)), b_heads, b_ex, b_tri,
        ],
        [
            like(rows, model, dtype=bf16), like(rows, conv_dim, dtype=bf16),
            like(rows, conv_dim, dtype=bf16), like(rows, conv_dim, dtype=bf16),
            lane_out, lane_out, lane_out, lane_out, like(rows, inner, dtype=bf16),
            like(16, conv_dim, dtype=bf16), like(LANES, inner + LANES, dtype=bf16), like(8, LANES),
        ],
        [
            b_model, b_act, b_act, b_act, b_lane, b_lane, b_lane, b_lane, b_in,
            full((16, conv_dim)), full((LANES, inner + LANES)), b_heads,
        ],
        [
            pltpu.VMEM((8 + SPAN, conv_dim), f32),
            pltpu.VMEM((LANES, inner), f32),
            pltpu.VMEM((8, LANES), f32),
        ],
        2 * rows * model * wide * 4,
        conv_dim=conv_dim,
        inner=inner,
        places=places,
    )

    def through(states, gains, reverse):
        whole = (places, LANES // places, inner)
        chained = call(
            chain_kernel, 1, [states, gains, ex],
            [full(states.shape), full(gains.shape), b_ex],
            [like(*whole, dtype=bf16)], [full(whole)], [], 1e7, reverse=reverse,
        )[0]
        return lax.all_to_all(chained, "seq", 0, 0, tiled=True).reshape(LANES, inner)

    arrived = lax.all_to_all(
        state_out.reshape(places, LANES // places, inner + LANES), "seq", 0, 0, tiled=True
    )
    gains = arrived[:, :2, inner:]
    prefix = through(arrived, gains, False)

    y_own, gate_in = call(
        intra_kernel,
        nblk,
        [act, dt_values, cumul, own_inc, normed, w_gate, ex],
        [b_act, b_lane, b_lane, b_in, b_model, full((model, inner)), b_ex],
        [like(rows, inner), like(rows, inner, dtype=bf16)],
        [b_in, b_in],
        [],
        2 * rows * model * inner * 4,
        inner=inner,
    )

    gated_low, grad_mixed, grad_gate, back_rows, r_sums, gdev, gate_sums = call(
        gate_kernel,
        nblk,
        [y_own, act, prefix, cumdev, meta, gate_in, w_out, cot, skip_wide, gate_gain, ex, red],
        [
            b_in, b_act, full((LANES, inner)), b_lane, b_meta, b_in, full((inner, model)), b_model,
            full((1, inner)), full((1, inner)), b_ex, b_red,
        ],
        [
            like(rows, inner, dtype=bf16), like(rows, inner, dtype=bf16), like(rows, inner, dtype=bf16),
            like(rows, model, dtype=bf16), lane_out, like(LANES, inner, dtype=bf16), like(16, inner),
        ],
        [b_in, b_in, b_in, b_model, b_lane, full((LANES, inner)), full((16, inner))],
        [pltpu.VMEM((SPAN, inner), f32)] * 4 + [pltpu.VMEM((LANES, inner), f32)],
        2 * rows * model * inner * 4,
        inner=inner,
    )

    above = through(
        lax.all_to_all(gdev.reshape(places, LANES // places, inner), "seq", 0, 0, tiled=True),
        gains, True,
    )

    flip = lambda i: nblk - 1 - i
    f_lane = rows_of(SPAN, LANES, flip)
    f_in = rows_of(SPAN, inner, flip)
    dx_own, dbc_own, xd_own, da_own = call(
        intra_back_kernel,
        nblk,
        [act, grad_mixed, dt_values, cumul, cumdev, meta, own_inc, prefix, r_sums, ex, red, tri_up],
        [
            rows_of(SPAN, conv_dim, flip), f_in, f_lane, f_lane, f_lane, rows_of(SPAN, 8, flip), f_in,
            full((LANES, inner)), f_lane, b_ex, b_red, b_tri,
        ],
        [like(rows, inner, dtype=bf16), like(rows, 2 * LANES), lane_out, lane_out],
        [f_in, rows_of(SPAN, 2 * LANES, flip), f_lane, f_lane],
        [pltpu.VMEM((LANES, inner), f32), pltpu.VMEM((8, LANES), f32)],
        2 * rows * model * inner * 6,
        inner=inner,
    )
    block_out, out_grad, gate_grad = call(
        outer_kernel,
        nblk,
        [u, meta, gated_low, back_rows, normed, grad_gate, w_out],
        [b_model, b_meta, b_in, b_model, b_model, b_in, full((inner, model))],
        [
            like(rows, model, dtype=bf16), like(inner, model, dtype=bf16),
            like(model, inner, dtype=bf16),
        ],
        [b_model, full((inner, model)), full((model, inner))],
        [pltpu.VMEM((inner, model), f32), pltpu.VMEM((model, inner), f32)],
        2 * rows * model * inner * 3,
    )
    out_sum = scatter_sum(out_grad)
    gate_sum = scatter_sum(gate_grad)

    capped = lambda i: jnp.minimum(i, nblk - 1)
    late = lambda i: jnp.maximum(i - 1, 0)
    c_lane = rows_of(SPAN, LANES, capped)
    c_in = rows_of(SPAN, inner, capped)
    c_act = rows_of(SPAN, conv_dim, capped)
    pre_last = jnp.broadcast_to(meta[rows - 1 :, 1:2], (8, LANES))
    dconv, first_rows, conv_sums, head_sum_rows = call(
        conv_back_kernel,
        nblk + 1,
        [
            act, slope, conv_in, dx_own, grad_mixed, dbc_own, dt_values, cumdev, raw, xd_own, da_own,
            meta, above, prefix, total, pre_last, skip_wide, taps, head_rows, rim, ex, red, tri,
        ],
        [
            c_act, c_act, c_act, c_in, c_in, rows_of(SPAN, 2 * LANES, capped), c_lane, c_lane, c_lane,
            c_lane, c_lane, rows_of(SPAN, 8, capped), full((LANES, inner)), full((LANES, inner)),
            b_heads, b_heads, full((1, inner)), full((4, conv_dim)), b_heads, full((16, conv_dim)),
            b_ex, b_red, b_tri,
        ],
        [
            like(rows, wide, dtype=bf16), like(8, conv_dim), like(40, conv_dim), like(16, LANES),
        ],
        [rows_of(SPAN, wide, late), full((8, conv_dim)), full((40, conv_dim)), full((16, LANES))],
        [
            pltpu.VMEM((SPAN, conv_dim), f32),
            pltpu.VMEM((SPAN + 8, conv_dim), f32),
            pltpu.VMEM((SPAN + 8, conv_dim), f32),
            pltpu.VMEM((SPAN, LANES), bf16),
            pltpu.VMEM((SPAN, LANES), bf16),
            pltpu.VMEM((8, LANES), f32),
        ],
        2 * rows * model * inner * 3,
        inner=inner,
        conv_dim=conv_dim,
        num_heads=heads,
    )

    after = shift(first_rows, "seq", -1)
    late_rows = jnp.stack(
        [sum(taps[k] * after[j - k] for k in range(j + 1)) for j in range(3)]
    )
    tail = dconv[rows - 16 :, :conv_dim].astype(f32) + jnp.pad(late_rows, ((13, 0), (0, 0)))
    dconv = lax.dynamic_update_slice(dconv, tail.astype(bf16), (rows - 16, 0))

    input_grad, norm_sums = call(
        input_grad_kernel,
        nblk,
        [dconv, grad_gate, w_conv, w_gate, u, cot, norm_gain],
        [
            rows_of(SPAN, wide), b_in, full((model, wide)), full((model, inner)), b_model, b_model,
            full((1, model)),
        ],
        [like(rows, model, dtype=bf16), like(8, model)],
        [b_model, full((8, model))],
        [],
        2 * rows * model * (wide + inner),
    )

    grad_taps = jnp.sum(conv_sums.reshape(5, 8, conv_dim), axis=1)
    grad_vecs = jnp.concatenate(
        [jnp.sum(norm_sums, axis=0), jnp.sum(gate_sums[:8], axis=0), grad_taps[4]]
    )
    grad_skip = jnp.sum(jnp.sum(gate_sums[8:], axis=0).reshape(heads, head_dim), axis=1)
    head_local = jnp.concatenate(
        [
            jnp.sum(head_sum_rows.reshape(2, 8, LANES), axis=1)[:, :heads].reshape(-1),
            grad_skip,
        ]
    )
    small_grads = jnp.concatenate(
        [
            grad_taps[:4].reshape(4, ranks, taps_own).transpose(1, 0, 2).reshape(ranks, 4 * taps_own),
            grad_vecs.reshape(ranks, vecs_own),
        ],
        axis=1,
    )
    small_grads = jnp.pad(small_grads, ((0, 0), (0, own_rows * spare - smalls)))
    small_grads = jnp.pad(small_grads.reshape(model, spare), ((0, 0), (heads, 0)))
    conv_grad = call(
        partial(weight_grad_kernel, conv_dim=conv_dim),
        nblk,
        [normed, dconv, small_grads],
        [b_model, rows_of(SPAN, wide), full((model, LANES))],
        [like(model, wide, dtype=bf16)],
        [full((model, wide))],
        [pltpu.VMEM((model, wide), f32)],
        2 * rows * model * wide,
    )[0]
    conv_all = scatter_sum(conv_grad)

    in_sum = jnp.concatenate([gate_sum, conv_all[:, : conv_dim + heads]], axis=1)
    small_sum = conv_all[:, conv_dim + heads :].reshape(-1)
    conv_sum = small_sum[: 4 * taps_own].reshape(4, taps_own)
    vec_sum = small_sum[4 * taps_own : smalls]
    owned_sq = (
        jnp.sum(in_sum * in_sum)
        + jnp.sum(out_sum * out_sum)
        + jnp.sum(conv_sum * conv_sum)
        + jnp.sum(vec_sum * vec_sum)
    )
    row = jnp.concatenate([head_local, owned_sq[None]])
    row = jnp.pad(row, (0, LANES - row.shape[0]))
    all_rows = lax.all_to_all(
        jnp.broadcast_to(row[None, None], (ranks, 1, LANES)), ("seq", "rep"), 0, 0, tiled=True
    )
    summed = jnp.sum(all_rows, axis=(0, 1))
    head_sum = summed[: 3 * heads].reshape(3, heads)
    norm_sq = summed[3 * heads] + jnp.sum(head_sum * head_sum)
    grad_norm = jnp.sqrt(norm_sq)
    factor = jnp.minimum(1.0, MAX_NORM / (grad_norm + 1e-06))
    results = [block_out[None], input_grad[None], grad_norm]
    for summed_grad, master, first, second, rate, decay in (
        (in_sum, in_weight, in_first, in_second, RATE_MAT, DECAY_MAT),
        (out_sum, out_weight, out_first, out_second, RATE_MAT, DECAY_MAT),
        (conv_sum, conv_weight, conv_first, conv_second, RATE_CONV, DECAY_MAT),
        (vec_sum, vectors, vec_first, vec_second, RATE_VEC, 0.0),
        (head_sum, head_params, head_first, head_second, RATE_HEAD, 0.0),
    ):
        clipped = summed_grad * factor
        results.append(clipped)
        results.extend(adam_step(master, clipped, first, second, rate, decay))
    return tuple(results)


def solution(mesh):
    tokens = P("rep", "seq", None)
    row_split = P(("seq", "rep"), None)
    column_split = P(None, ("seq", "rep"))
    flat_split = P(("seq", "rep"))
    return jax.shard_map(
        shards,
        mesh=mesh,
        in_specs=(tokens, tokens, P("rep", None))
        + (row_split,) * 6
        + (column_split,) * 3
        + (flat_split,) * 3
        + (P(),) * 3,
        out_specs=(tokens, tokens, P())
        + (row_split,) * 10
        + (column_split,) * 5
        + (flat_split,) * 5
        + (P(),) * 5,
        check_vma=False,
    )
```

time: 909 us -> 452 us (0.50)
  matrix products: 241 us -> 0 us
  Pallas kernels: 0 us -> 215 us
  other arithmetic: 246 us -> 31.5 us
  blocking collectives: 180 us -> 10.5 us
  local copies, waits for them, and re-layouts: 126 us -> 28.3 us
  starting transfers between devices: 3.75 us -> 50.2 us
  waiting for transfers between devices: 73.2 us -> 86.3 us
    dot_general x54 -> x0, matrix products: 241 us -> none  [the longest x6 25 us: intra_forward(): jnp.einsum('hts,shp->thp', weights.astype(jnp.bfloat16), x_rows, preferre...]
    pallas_call x0 -> x10, Pallas kernels: none -> 215 us  [call(): pl.pallas_call(partial(kernel, **fixed), grid=(grid,), in_specs=in_blocks...]
    all_gather x3 -> x0, blocking collectives: 98.5 us -> none  [the longest x1 43.1 us: shards(): lax.all_gather(vectors.astype(jnp.bfloat16), ('seq', 'rep'), axis=0, tile...]
    unnamed x7 -> x2, waiting for transfers between devices: 70.7 us -> 0.03 us
    ppermute x2 -> x22, waiting for transfers between devices: 2.46 us -> 68.3 us  [the longest x20 64.6 us: swap(): return lax.ppermute(value, axis, [(k, k ^ bit) for k in range(count)])]
    reduce_sum x13 -> x7, other arithmetic: 62.1 us -> 3.78 us  [the longest x1 1.04 us: shards(): grad_taps = jnp.sum(conv_sums.reshape(5, 8, conv_dim), axis=1)]
    unnamed x1 -> x0, blocking collectives: 42.1 us -> none
    another operation x16 -> x9, other arithmetic: 43.3 us -> 2.54 us
  transfers between devices with their start and end apart: 8 -> 28, of which waited for: 2 -> 13; matrix products, arithmetic and copies ran while one was open for 53% -> 11% of each run, Pallas kernels for 0% -> 42%
where the time goes in v1:
time: 452 us; the launch traced here: 443 us
  Pallas kernels  215 us (48%)
  waiting for transfers between devices  86.3 us (19%)
  starting transfers between devices  50.2 us (11%)
  other arithmetic  31.5 us (7%)
  local copies, waits for them, and re-layouts  28.3 us (6%)
  between operations  21 us (5%)
  blocking collectives  10.5 us (2%)
    pallas_call x10, Pallas kernels, call(): pl.pallas_call(partial(kernel, **fixed), grid=(grid,), in_specs=in_blocks...  215 us
    ppermute x20, waiting for transfers between devices, swap(): return lax.ppermute(value, axis, [(k, k ^ bit) for k in range(count)])  64.6 us
    ppermute x20, starting transfers between devices, swap(): return lax.ppermute(value, axis, [(k, k ^ bit) for k in range(count)])  19.5 us
    all_to_all x1, waiting for transfers between devices, shards(): lax.all_to_all(state_out.reshape(places, LANES // places, inner + LANES),...  12.5 us
    all_to_all x1, blocking collectives, shards(): lax.all_to_all(jnp.broadcast_to(row[None, None], (ranks, 1, LANES)), ('se...  10.5 us
    all_to_all x2, starting transfers between devices, through(): lax.all_to_all(chained, 'seq', 0, 0, tiled=True).reshape(LANES, inner)  10.2 us
  transfers between devices with their start and end apart: 28, of which 13 were waited for; matrix products, arithmetic and copies ran while one was open for 11% of the time, Pallas kernels for 42%

profile of v1, /device:TPU:0, one launch (start us, length us, event | category | flops | bytes accessed | tf_op | source)
XLA Modules:
  0.0 443.0 jit_solution(4833571217471950790)
XLA Ops:
  7.3 1.0 convert_element_type.299
  9.7 4.9 %collective-permute-start = (bf16[16,768]{1,0:T(8,128)(2,1)S(1)}, bf16[16,768]{1,0:T(8,128)(2,1)S(1)}, u32[]{:S(2)}, u32[]{:S(2)}) collective-permute-start(bf16[16,768]{1,0:T(8,128)(2,1)S(1)} %slice_bitcast_fusion), channel_id=1, source_target_pairs={{0,4},{4,8},{8,12},{12,16},{16,20},{20,24},{24,28},{1,5},{5,9},{9,... | collective-permute-start | bytes 73736 | tf_op jit(solution)/shard_map/ppermute | solution.py:534
  16.3 2.6 collective-permute-start.1
  18.9 1.6 convert_element_type.303
  21.1 2.2 collective-permute-done.1
  24.2 5.0 %collective-permute-done.2 = bf16[2,24,1920]{2,1,0:T(8,128)(2,1)S(1)} collective-permute-done((bf16[2,24,1920]{2,1,0:T(8,128)(2,1)S(1)}, bf16[2,24,1920]{2,1,0:T(8,128)(2,1)S(1)}, u32[]{:S(2)}, u32[]{:S(2)}) %collective-permute-start.2) | collective-permute-done | bytes 184352 | tf_op jit(solution)/shard_map/ppermute | solution.py:543
  29.2 1.6 collective-permute-start.3
  30.9 6.9 %collective-permute-done.3 = bf16[2,2,24,1920]{3,2,0,1:T(8,128)(2,1)S(1)} collective-permute-done((bf16[2,2,24,1920]{3,2,0,1:T(8,128)(2,1)S(1)}, bf16[2,2,24,1920]{3,2,0,1:T(8,128)(2,1)S(1)}, u32[]{:S(2)}, u32[]{:S(2)}) %collective-permute-start.3) | collective-permute-done | bytes 368672 | tf_op jit(solution)/shard_map/ppermute | solution.py:543
  37.9 1.9 collective-permute-start.4
  41.3 14.6 %collective-permute-done.4 = bf16[2,2,2,24,1920]{4,3,0,1,2:T(8,128)(2,1)S(1)} collective-permute-done((bf16[2,2,2,24,1920]{4,3,0,1,2:T(8,128)(2,1)S(1)}, bf16[2,2,2,24,1920]{4,3,0,1,2:T(8,128)(2,1)S(1)}, u32[]{:S(2)}, u32[]{:S(2)}) %collective-permute-start.4) | collective-permute-done | bytes 737312 | tf_op jit(solution)/shard_map/ppermute | solution.py:543
  58.4 1.2 copy.109.meta_ref
  60.9 1.0 add_convert_fusion.ex_ref
  62.3 2.4 maximum_select_fusion
  65.1 1.1 reshape.776
  66.2 0.8 slice_bitcast_fusion.2
  67.0 0.8 slice_bitcast_fusion.3
  71.2 30.9 %shard_map.393 = (bf16[1536,768]{1,0:T(8,128)(2,1)}, bf16[1536,1792]{1,0:T(8,128)(2,1)}, bf16[1536,1792]{1,0:T(8,128)(2,1)}, bf16[1536,1792]{1,0:T(8,128)(2,1)},...) custom-call(bf16[1536,768]{1,0:T(8,128)(2,1)} %bitcast.196, ...), custom_call_target="tpu_custom_call" | custom-call | flops 18119393280 | bytes 33470464 | tf_op jit(solution)/shard_map/pallas_call | solution.py:585
  102.1 7.8 %all-to-all-start = ((bf16[8,16,1664]{2,1,0:T(8,128)(2,1)}), bf16[8,16,1664]{2,1,0:T(8,128)(2,1)S(1)}, u32[]{:S(2)}, u32[]{:S(2)}) async-start(bf16[8,16,1664]{2,1,0:T(8,128)(2,1)} %bitcast.184), calls=%async_computation | async-start | bytes 851968 | tf_op jit(solution)/shard_map/all_to_all | solution.py:742
  109.9 1.0 fusion.6.red_ref
  110.9 0.8 slice_bitcast_fusion.1
  114.0 12.5 %all-to-all-done.states_ref = bf16[8,16,1664]{2,1,0:T(8,128)(2,1)S(1)} async-done(((bf16[8,16,1664]{2,1,0:T(8,128)(2,1)}), bf16[8,16,1664]{2,1,0:T(8,128)(2,1)S(1)}, u32[]{:S(2)}, u32[]{:S(2)}) %all-to-all-start) | async-done | bytes 426016 | tf_op jit(solution)/shard_map/all_to_all | solution.py:742
  127.2 2.3 shard_map.395
  129.4 4.0 all-to-all-start.1
  133.5 24.1 %shard_map.394 = (f32[1536,1536]{1,0:T(8,128)}, bf16[1536,1536]{1,0:T(8,128)(2,1)}) custom-call(bf16[1536,1792]{1,0:T(8,128)(2,1)} %get-tuple-element.62.act_ref, f32[1536,128]{1,0:T(8,128)} %get-tuple-element.63.dt_ref, f32[1536,128]{1,0:T(8,128)} %get-tuple-element.64.cum_ref, bf16[1536,1536]{1,0:T(8,128)(2,1)} %get-tuple-element.65.inc_ref, ...), custom_call_target="tpu_custom_call" | custom-call | flops 14495514624 | bytes 31457280 | tf_op jit(solution)/shard_map/pallas_call | solution.py:585
  158.3 27.3 %shard_map.396 = (bf16[1536,1536]{1,0:T(8,128)(2,1)}, bf16[1536,1536]{1,0:T(8,128)(2,1)}, bf16[1536,1536]{1,0:T(8,128)(2,1)}, bf16[1536,768]{1,0:T(8,128)(2,1)},...) custom-call(f32[1536,1536]{1,0:T(8,128)} %get-tuple-element.67.y_ref, ...), custom_call_target="tpu_custom_call" | custom-call | flops 14495514624 | bytes 44593152 | tf_op jit(solution)/shard_map/pallas_call | solution.py:585
  185.6 6.1 %all-to-all-start.2 = ((bf16[8,16,1536]{2,1,0:T(8,128)(2,1)}), bf16[8,16,1536]{2,1,0:T(8,128)(2,1)S(1)}, u32[]{:S(2)}, u32[]{:S(2)}) async-start(bf16[8,16,1536]{2,1,0:T(8,128)(2,1)} %bitcast.188), calls=%async_computation.2 | async-start | bytes 786432 | tf_op jit(solution)/shard_map/all_to_all | solution.py:779
  191.7 18.5 %shard_map.397 = (bf16[1536,768]{1,0:T(8,128)(2,1)}, bf16[1536,768]{1,0:T(8,128)(2,1)}, bf16[768,1536]{1,0:T(8,128)(2,1)}) custom-call(bf16[1536,768]{1,0:T(8,128)(2,1)} %bitcast.197, f32[1536,8]{1,0:T(8,128)} %copy.109.meta_ref, bf16[1536,1536]{1,0:T(8,128)(2,1)} %get-tuple-element.71.low_ref, bf16[1536,768]{1,0:T(8,128)(2,1)} %get-tuple-element.72.back_ref, ...), custom_call_target="tpu_custom_call" | custom-call | flops 10871635968 | bytes 26001408 | tf_op jit(solution)/shard_map/pallas_call | solution.py:585
  210.2 1.9 constant_dynamic-slice_fusion.5
  212.1 1.1 copy.143
  213.3 1.0 copy-done.1
  214.4 1.1 copy.142
  215.5 47.9 %shard_map.398 = (bf16[1536,1536]{1,0:T(8,128)(2,1)}, f32[1536,256]{1,0:T(8,128)}, f32[1536,128]{1,0:T(8,128)}, f32[1536,128]{1,0:T(8,128)}) custom-call(bf16[1536,1792]{1,0:T(8,128)(2,1)} %get-tuple-element.62.act_ref, bf16[1536,1536]{1,0:T(8,128)(2,1)} %get-tuple-element.77.gm_ref, f32[1536,128]{1,0:T(8,128)} %get-tuple-element.63.dt_ref, ...), custom_call_target="tpu_custom_call" | custom-call | flops 21743271936 | bytes 27607040 | tf_op jit(solution)/shard_map/pallas_call | solution.py:585
  264.9 2.3 shard_map.399
  267.2 6.3 %all-to-all-start.3 = ((bf16[8,16,1536]{2,1,0:T(8,128)(2,1)}), bf16[8,16,1536]{2,1,0:T(8,128)(2,1)}, u32[]{:S(2)}, u32[]{:S(2)}) async-start(bf16[8,16,1536]{2,1,0:T(8,128)(2,1)} %shard_map.399), calls=%async_computation.3 | async-start | bytes 786432 | tf_op jit(solution)/shard_map/all_to_all | solution.py:740
  273.5 1.6 fusion.2
  275.0 0.9 dynamic-slice_bitcast_fusion.2
  276.1 1.5 fusion.1
  277.6 0.9 dynamic-slice_bitcast_fusion.1
  278.5 1.8 collective-permute-start.18
  280.4 5.5 %all-to-all-done.3 = bf16[8,16,1536]{2,1,0:T(8,128)(2,1)} async-done(((bf16[8,16,1536]{2,1,0:T(8,128)(2,1)}), bf16[8,16,1536]{2,1,0:T(8,128)(2,1)}, u32[]{:S(2)}, u32[]{:S(2)}) %all-to-all-start.3) | async-done | bytes 393248 | tf_op jit(solution)/shard_map/all_to_all | solution.py:740
  286.4 36.0 %shard_map.400 = (bf16[1536,1920]{1,0:T(8,128)(2,1)}, f32[8,1792]{1,0:T(8,128)}, f32[40,1792]{1,0:T(8,128)}, f32[16,128]{1,0:T(8,128)}) custom-call(bf16[1536,1792]{1,0:T(8,128)(2,1)} %get-tuple-element.62.act_ref, bf16[1536,1792]{1,0:T(8,128)(2,1)} %get-tuple-element.75.slope_ref, bf16[1536,1792]{1,0:T(8,128)(2,1)} %get-tuple-element.76.conv_ref, ...), custom_call_target="tpu_custom_call" | custom-call | flops 10871635968 | bytes 39860224 | tf_op jit(solution)/shard_map/pallas_call | solution.py:585
  322.5 1.0 bitcast_reduce_fusion
  323.5 1.5 collective-permute-start.6
  326.2 3.7 collective-permute-done.6
  329.9 1.5 fusion.26.dconv_ref
  331.3 15.4 %shard_map.401 = (bf16[1536,768]{1,0:T(8,128)(2,1)}, f32[8,768]{1,0:T(8,128)}) custom-call(bf16[1536,1920]{1,0:T(8,128)(2,1)} %fusion.26.dconv_ref, bf16[1536,1536]{1,0:T(8,128)(2,1)} %get-tuple-element.73.dgate_ref, bf16[768,1920]{1,0:T(8,128)(2,1)} %bitcast.164, bf16[768,1536]{1,0:T(8,128)(2,1)} %all-gather.3.cloned.1.call-done.w_ref.wg_ref, ...), custom_call_target="tpu_custom_call" | custom-call | flops 8153726976 | bytes 23030784 | tf_op jit(solution)/shard_map/pallas_call | solution.py:585
  347.8 0.9 pad.28.small_ref
  348.8 10.6 %shard_map.402 = bf16[768,1920]{1,0:T(8,128)(2,1)} custom-call(bf16[1536,768]{1,0:T(8,128)(2,1)} %get-tuple-element.66.normed_ref, bf16[1536,1920]{1,0:T(8,128)(2,1)} %fusion.26.dconv_ref, f32[768,128]{1,0:T(8,128)} %pad.28.small_ref), custom_call_target="tpu_custom_call" | custom-call | flops 4529848320 | bytes 11599872 | tf_op jit(solution)/shard_map/pallas_call | solution.py:585
  359.3 2.0 constant_dynamic-slice_fusion.3
  361.6 1.2 fusion.5
  362.8 2.4 collective-permute-start.9
  365.3 1.2 fusion.4
  366.6 6.5 %collective-permute-done.9 = bf16[2,2,24,1536]{3,2,0,1:T(8,128)(2,1)S(1)} collective-permute-done((bf16[2,2,24,1536]{3,2,0,1:T(8,128)(2,1)S(1)}, bf16[2,2,24,1536]{3,2,0,1:T(8,128)(2,1)S(1)}, u32[]{:S(2)}, u32[]{:S(2)}) %collective-permute-start.9) | collective-permute-done | bytes 294944 | tf_op jit(solution)/shard_map/ppermute | solution.py:543
  374.6 4.7 %collective-permute-done.19 = bf16[2,2,48,768]{3,2,0,1:T(8,128)(2,1)S(1)} collective-permute-done((bf16[2,2,48,768]{3,2,0,1:T(8,128)(2,1)S(1)}, bf16[2,2,48,768]{3,2,0,1:T(8,128)(2,1)S(1)}, u32[]{:S(2)}, u32[]{:S(2)}) %collective-permute-start.19) | collective-permute-done | bytes 294944 | tf_op jit(solution)/shard_map/ppermute | solution.py:543
  379.8 12.2 %collective-permute-done.13 = bf16[2,2,2,24,1920]{4,3,0,1,2:T(8,128)(2,1)S(1)} collective-permute-done((bf16[2,2,2,24,1920]{4,3,0,1,2:T(8,128)(2,1)S(1)}, bf16[2,2,2,24,1920]{4,3,0,1,2:T(8,128)(2,1)S(1)}, u32[]{:S(2)}, u32[]{:S(2)}) %collective-permute-start.13) | collective-permute-done | bytes 737312 | tf_op jit(solution)/shard_map/ppermute | solution.py:543
  392.2 1.6 collective-permute-start.14
  393.9 3.0 collective-permute-start.21
  396.9 4.2 collective-permute-done.14
  401.2 2.0 collective-permute-start.15
  403.3 3.7 collective-permute-done.15
  408.0 4.6 %collective-permute-done.16 = bf16[24,1920]{1,0:T(8,128)(2,1)S(1)} collective-permute-done((bf16[24,1920]{1,0:T(8,128)(2,1)S(1)}, bf16[24,1920]{1,0:T(8,128)(2,1)S(1)}, u32[]{:S(2)}, u32[]{:S(2)}) %collective-permute-start.16) | collective-permute-done | bytes 92192 | tf_op jit(solution)/shard_map/ppermute | solution.py:543
  417.5 10.5 %all_to_all.25 = f32[32,1,128]{2,1,0:T(1,128)S(1)} all-to-all(f32[32,1,128]{2,1,0:T(1,128)S(1)} %broadcast_in_dim.71), channel_id=1, replica_groups=mesh['seq'=8,'rep'=4] {'seq','rep'}, dimensions={0} | all-to-all | bytes 32768 | tf_op jit(solution)/shard_map/all_to_all | solution.py:918
  431.5 1.2 fusion.51
  433.9 0.9 fusion.49
  (200 shorter events, 31.2 us)
Async XLA Ops:
  7.2 13.5 %copy-start.27 = (s32[1,3]{1,0:T(1,128)S(1)}, s32[1,3]{1,0:T(1,128)}, u32[]{:S(2)}) copy-start(s32[1,3]{1,0:T(1,128)} %param.20) | copy-start | bytes 40
  7.2 13.7 %copy-start.17 = (f32[3,24]{1,0:T(4,128)S(1)}, f32[3,24]{1,0:T(4,128)}, u32[]{:S(2)}) copy-start(f32[3,24]{1,0:T(4,128)} %param.33) | copy-start | bytes 868
  7.2 126.2 %all-gather.3.cloned.1.call-start = ((), (), s32[]{:S(2)}) async-start(), calls=%async_computation.5 | async-start | bytes 2433024 | tf_op jit(solution)/shard_map/all_gather | solution.py:669
  8.9 148.7 %all-gather.5.cloned.1.call-start = ((), (), s32[]{:S(2)}) async-start(), calls=%async_computation.6 | async-start | bytes 2433024 | tf_op jit(solution)/shard_map/all_gather | solution.py:670
  9.7 60.8 %collective-permute-start = (bf16[16,768]{1,0:T(8,128)(2,1)S(1)}, bf16[16,768]{1,0:T(8,128)(2,1)S(1)}, u32[]{:S(2)}, u32[]{:S(2)}) collective-permute-start(bf16[16,768]{1,0:T(8,128)(2,1)S(1)} %slice_bitcast_fusion), channel_id=1, source_target_pairs={{0,4},{4,8},{8,12},{12,16},{16,20},{20,24},{24,28},{1,5},{5,9},{9,... | collective-permute-start | bytes 73736 | tf_op jit(solution)/shard_map/ppermute | solution.py:534
  16.3 7.0 %collective-permute-start.1 = (bf16[24,1920]{1,0:T(8,128)(2,1)S(1)}, bf16[24,1920]{1,0:T(8,128)(2,1)S(1)}, u32[]{:S(2)}, u32[]{:S(2)}) collective-permute-start(bf16[24,1920]{1,0:T(8,128)(2,1)S(1)} %pad_maximum_fusion.1), channel_id=1, source_target_pairs={{0,16},{4,20},{8,24},{12,28},{16,0},{20,4},{24,8},{28,12},{1,17},{... | collective-permute-start | bytes 276488 | tf_op jit(solution)/shard_map/ppermute | solution.py:543
  23.4 5.8 %collective-permute-start.2 = (bf16[2,24,1920]{2,1,0:T(8,128)(2,1)S(1)}, bf16[2,24,1920]{2,1,0:T(8,128)(2,1)S(1)}, u32[]{:S(2)}, u32[]{:S(2)}) collective-permute-start(bf16[2,24,1920]{2,1,0:T(8,128)(2,1)S(1)} %maximum_select_fusion.8), channel_id=1, source_target_pairs={{0,8},{4,12},{8,0},{12,4},{16,24},{20,28},{24,16},{28,20},{1,9},{5... | collective-permute-start | bytes 552968 | tf_op jit(solution)/shard_map/ppermute | solution.py:543
  29.2 8.5 %collective-permute-start.3 = (bf16[2,2,24,1920]{3,2,0,1:T(8,128)(2,1)S(1)}, bf16[2,2,24,1920]{3,2,0,1:T(8,128)(2,1)S(1)}, u32[]{:S(2)}, u32[]{:S(2)}) collective-permute-start(bf16[2,2,24,1920]{3,2,0,1:T(8,128)(2,1)S(1)} %maximum_select_fusion.6), channel_id=1, source_target_pairs={{0,4},{4,0},{8,12},{12,8},{16,20},{20,16},{24,28},{28,24},{1,5},{5... | collective-permute-start | bytes 1105928 | tf_op jit(solution)/shard_map/ppermute | solution.py:543
  37.9 18.0 %collective-permute-start.4 = (bf16[2,2,2,24,1920]{4,3,0,1,2:T(8,128)(2,1)S(1)}, bf16[2,2,2,24,1920]{4,3,0,1,2:T(8,128)(2,1)S(1)}, u32[]{:S(2)}, u32[]{:S(2)}) collective-permute-start(bf16[2,2,2,24,1920]{4,3,0,1,2:T(8,128)(2,1)S(1)} %maximum_select_fusion.4), channel_id=1, source_target_pairs={{0,2},{1,3},{2,0},{3,1},{4,6},{5,7},{6,4},{7,5},{8,10},{9,11},{10,... | collective-permute-start | bytes 2211848 | tf_op jit(solution)/shard_map/ppermute | solution.py:543
  56.2 6.1 %collective-permute-start.5 = (bf16[2,2,2,2,24,1920]{5,4,0,1,2,3:T(8,128)(2,1)S(1)}, bf16[2,2,2,2,24,1920]{5,4,0,1,2,3:T(8,128)(2,1)}, u32[]{:S(2)}, u32[]{:S(2)}) collective-permute-start(bf16[2,2,2,2,24,1920]{5,4,0,1,2,3:T(8,128)(2,1)S(1)} %maximum_select_fusion.2), channel_id=1, source_target_pairs={{0,1},{1,0},{2,3},{3,2},{4,5},{5,4},{6,7},{7,6},{8,9},{9,8},{10,11... | collective-permute-start | bytes 4423688 | tf_op jit(solution)/shard_map/ppermute | solution.py:543
  64.9 5.6 %copy-start = (bf16[2,2,2,2,2,24,1920]{6,5,4,3,2,1,0:T(8,128)(2,1)}, bf16[2,2,2,2,2,24,1920]{6,5,4,3,2,1,0:T(8,128)(2,1)S(1)}, u32[]{:S(2)}) copy-start(bf16[2,2,2,2,2,24,1920]{6,5,4,3,2,1,0:T(8,128)(2,1)S(1)} %copy.105) | copy-start | bytes 8847364
  70.6 0.6 copy-start.28
  102.1 24.3 %all-to-all-start = ((bf16[8,16,1664]{2,1,0:T(8,128)(2,1)}), bf16[8,16,1664]{2,1,0:T(8,128)(2,1)S(1)}, u32[]{:S(2)}, u32[]{:S(2)}) async-start(bf16[8,16,1664]{2,1,0:T(8,128)(2,1)} %bitcast.184), calls=%async_computation | async-start | bytes 851968 | tf_op jit(solution)/shard_map/all_to_all | solution.py:742
  126.4 0.8 copy-start.2
  129.4 28.1 %all-to-all-start.1 = ((bf16[8,16,1536]{2,1,0:T(8,128)(2,1)}), bf16[8,16,1536]{2,1,0:T(8,128)(2,1)S(1)}, u32[]{:S(2)}, u32[]{:S(2)}) async-start(bf16[8,16,1536]{2,1,0:T(8,128)(2,1)} %shard_map.395), calls=%async_computation.1 | async-start | bytes 786432 | tf_op jit(solution)/shard_map/all_to_all | solution.py:740
  157.6 0.7 copy-start.6
  185.6 78.5 %all-to-all-start.2 = ((bf16[8,16,1536]{2,1,0:T(8,128)(2,1)}), bf16[8,16,1536]{2,1,0:T(8,128)(2,1)S(1)}, u32[]{:S(2)}, u32[]{:S(2)}) async-start(bf16[8,16,1536]{2,1,0:T(8,128)(2,1)} %bitcast.188), calls=%async_computation.2 | async-start | bytes 786432 | tf_op jit(solution)/shard_map/all_to_all | solution.py:779
  212.1 2.1 copy-start.1
  213.3 60.2 %collective-permute-start.7 = (bf16[2,2,2,2,24,1536]{5,4,0,1,2,3:T(8,128)(2,1)}, bf16[2,2,2,2,24,1536]{5,4,0,1,2,3:T(8,128)(2,1)}, u32[]{:S(2)}, u32[]{:S(2)}) collective-permute-start(bf16[2,2,2,2,24,1536]{5,4,0,1,2,3:T(8,128)(2,1)} %bitcast.156), channel_id=1, source_target_pairs={{0,1},{1,0},{2,3},{3,2},{4,5},{5,4},{6,7},{7,6},{8,9},{9,8},{10,11... | collective-permute-start | bytes 3538952 | tf_op jit(solution)/shard_map/ppermute | solution.py:543
  215.5 60.6 %collective-permute-start.17 = (bf16[2,2,2,2,48,768]{5,4,0,1,2,3:T(8,128)(2,1)}, bf16[2,2,2,2,48,768]{5,4,0,1,2,3:T(8,128)(2,1)}, u32[]{:S(2)}, u32[]{:S(2)}) collective-permute-start(bf16[2,2,2,2,48,768]{5,4,0,1,2,3:T(8,128)(2,1)} %bitcast.155), channel_id=1, source_target_pairs={{0,1},{1,0},{2,3},{3,2},{4,5},{5,4},{6,7},{7,6},{8,9},{9,8},{10,11... | collective-permute-start | bytes 3538952 | tf_op jit(solution)/shard_map/ppermute | solution.py:543
  215.5 47.9 %copy-start.11 = (f32[16,1536]{1,0:T(8,128)S(1)}, f32[16,1536]{1,0:T(8,128)}, u32[]{:S(2)}) copy-start(f32[16,1536]{1,0:T(8,128)} %get-tuple-element.91) | copy-start | bytes 294916
  264.1 0.8 copy-start.3
  267.2 18.6 %all-to-all-start.3 = ((bf16[8,16,1536]{2,1,0:T(8,128)(2,1)}), bf16[8,16,1536]{2,1,0:T(8,128)(2,1)}, u32[]{:S(2)}, u32[]{:S(2)}) async-start(bf16[8,16,1536]{2,1,0:T(8,128)(2,1)} %shard_map.399), calls=%async_computation.3 | async-start | bytes 786432 | tf_op jit(solution)/shard_map/all_to_all | solution.py:740
  275.9 85.7 %collective-permute-start.8 = (bf16[2,2,2,24,1536]{4,3,0,1,2:T(8,128)(2,1)}, bf16[2,2,2,24,1536]{4,3,0,1,2:T(8,128)(2,1)}, u32[]{:S(2)}, u32[]{:S(2)}) collective-permute-start(bf16[2,2,2,24,1536]{4,3,0,1,2:T(8,128)(2,1)} %dynamic-slice_bitcast_fusion.2), channel_id=1, source_target_pairs={{0,2},{1,3},{2,0},{3,1},{4,6},{5,7},{6,4},{7,5},{8,10},{9,11},{10,... | collective-permute-start | bytes 1769480 | tf_op jit(solution)/shard_map/ppermute | solution.py:543
  278.5 86.8 %collective-permute-start.18 = (bf16[2,2,2,48,768]{4,3,0,1,2:T(8,128)(2,1)}, bf16[2,2,2,48,768]{4,3,0,1,2:T(8,128)(2,1)}, u32[]{:S(2)}, u32[]{:S(2)}) collective-permute-start(bf16[2,2,2,48,768]{4,3,0,1,2:T(8,128)(2,1)} %dynamic-slice_bitcast_fusion.1), channel_id=1, source_target_pairs={{0,2},{1,3},{2,0},{3,1},{4,6},{5,7},{6,4},{7,5},{8,10},{9,11},{10,... | collective-permute-start | bytes 1769480 | tf_op jit(solution)/shard_map/ppermute | solution.py:543
  286.4 43.4 %copy-start.12 = (f32[1,1792]{1,0:T(1,128)S(1)}, f32[1,1792]{1,0:T(1,128)}, u32[]{:S(2)}) copy-start(f32[1,1792]{1,0:T(1,128)} %squeeze.119) | copy-start | bytes 21508
  286.4 43.4 %copy-start.13 = (f32[1,1792]{1,0:T(1,128)S(1)}, f32[1,1792]{1,0:T(1,128)}, u32[]{:S(2)}) copy-start(f32[1,1792]{1,0:T(1,128)} %squeeze.117) | copy-start | bytes 21508
  323.5 6.3 %collective-permute-start.6 = (f32[8,1792]{1,0:T(8,128)}, f32[8,1792]{1,0:T(8,128)S(1)}, u32[]{:S(2)}, u32[]{:S(2)}) collective-permute-start(f32[8,1792]{1,0:T(8,128)} %get-tuple-element.88), channel_id=1, source_target_pairs={{4,0},{8,4},{12,8},{16,12},{20,16},{24,20},{28,24},{5,1},{9,5},{13... | collective-permute-start | bytes 172040 | tf_op jit(solution)/shard_map/ppermute | solution.py:534
  361.5 12.3 %collective-permute-start.12 = (bf16[2,2,2,2,24,1920]{5,4,0,1,2,3:T(8,128)(2,1)S(1)}, bf16[2,2,2,2,24,1920]{5,4,0,1,2,3:T(8,128)(2,1)S(1)}, u32[]{:S(2)}, u32[]{:S(2)}) collective-permute-start(bf16[2,2,2,2,24,1920]{5,4,0,1,2,3:T(8,128)(2,1)S(1)} %bitcast.178), channel_id=1, source_target_pairs={{0,1},{1,0},{2,3},{3,2},{4,5},{5,4},{6,7},{7,6},{8,9},{9,8},{10,11... | collective-permute-start | bytes 4423688 | tf_op jit(solution)/shard_map/ppermute | solution.py:543
  362.8 10.3 %collective-permute-start.9 = (bf16[2,2,24,1536]{3,2,0,1:T(8,128)(2,1)S(1)}, bf16[2,2,24,1536]{3,2,0,1:T(8,128)(2,1)S(1)}, u32[]{:S(2)}, u32[]{:S(2)}) collective-permute-start(bf16[2,2,24,1536]{3,2,0,1:T(8,128)(2,1)S(1)} %dynamic-slice_bitcast_fusion.5), channel_id=1, source_target_pairs={{0,4},{4,0},{8,12},{12,8},{16,20},{20,16},{24,28},{28,24},{1,5},{5... | collective-permute-start | bytes 884744 | tf_op jit(solution)/shard_map/ppermute | solution.py:543
  366.5 12.7 %collective-permute-start.19 = (bf16[2,2,48,768]{3,2,0,1:T(8,128)(2,1)S(1)}, bf16[2,2,48,768]{3,2,0,1:T(8,128)(2,1)S(1)}, u32[]{:S(2)}, u32[]{:S(2)}) collective-permute-start(bf16[2,2,48,768]{3,2,0,1:T(8,128)(2,1)S(1)} %dynamic-slice_bitcast_fusion.4), channel_id=1, source_target_pairs={{0,4},{4,0},{8,12},{12,8},{16,20},{20,16},{24,28},{28,24},{1,5},{5... | collective-permute-start | bytes 884744 | tf_op jit(solution)/shard_map/ppermute | solution.py:543
  373.2 6.5 %collective-permute-start.10 = (bf16[2,24,1536]{2,1,0:T(8,128)(2,1)S(1)}, bf16[2,24,1536]{2,1,0:T(8,128)(2,1)S(1)}, u32[]{:S(2)}, u32[]{:S(2)}) collective-permute-start(bf16[2,24,1536]{2,1,0:T(8,128)(2,1)S(1)} %dynamic-slice_bitcast_fusion.8), channel_id=1, source_target_pairs={{0,8},{4,12},{8,0},{12,4},{16,24},{20,28},{24,16},{28,20},{1,9},{5... | collective-permute-start | bytes 442376 | tf_op jit(solution)/shard_map/ppermute | solution.py:543
  374.3 17.7 %collective-permute-start.13 = (bf16[2,2,2,24,1920]{4,3,0,1,2:T(8,128)(2,1)S(1)}, bf16[2,2,2,24,1920]{4,3,0,1,2:T(8,128)(2,1)S(1)}, u32[]{:S(2)}, u32[]{:S(2)}) collective-permute-start(bf16[2,2,2,24,1920]{4,3,0,1,2:T(8,128)(2,1)S(1)} %dynamic-slice_bitcast_fusion), channel_id=1, source_target_pairs={{0,2},{1,3},{2,0},{3,1},{4,6},{5,7},{6,4},{7,5},{8,10},{9,11},{10,... | collective-permute-start | bytes 2211848 | tf_op jit(solution)/shard_map/ppermute | solution.py:543
  379.4 14.5 %collective-permute-start.20 = (bf16[2,48,768]{2,1,0:T(8,128)(2,1)S(1)}, bf16[2,48,768]{2,1,0:T(8,128)(2,1)S(1)}, u32[]{:S(2)}, u32[]{:S(2)}) collective-permute-start(bf16[2,48,768]{2,1,0:T(8,128)(2,1)S(1)} %dynamic-slice_bitcast_fusion.7), channel_id=1, source_target_pairs={{0,8},{4,12},{8,0},{12,4},{16,24},{20,28},{24,16},{28,20},{1,9},{5... | collective-permute-start | bytes 442376 | tf_op jit(solution)/shard_map/ppermute | solution.py:543
  392.2 8.8 %collective-permute-start.14 = (bf16[2,2,24,1920]{3,2,0,1:T(8,128)(2,1)S(1)}, bf16[2,2,24,1920]{3,2,0,1:T(8,128)(2,1)S(1)}, u32[]{:S(2)}, u32[]{:S(2)}) collective-permute-start(bf16[2,2,24,1920]{3,2,0,1:T(8,128)(2,1)S(1)} %dynamic-slice_bitcast_fusion.3), channel_id=1, source_target_pairs={{0,4},{4,0},{8,12},{12,8},{16,20},{20,16},{24,28},{28,24},{1,5},{5... | collective-permute-start | bytes 1105928 | tf_op jit(solution)/shard_map/ppermute | solution.py:543
  393.8 9.4 %collective-permute-start.11 = (bf16[24,1536]{1,0:T(8,128)(2,1)S(1)}, bf16[24,1536]{1,0:T(8,128)(2,1)S(1)}, u32[]{:S(2)}, u32[]{:S(2)}) collective-permute-start(bf16[24,1536]{1,0:T(8,128)(2,1)S(1)} %dynamic-slice_bitcast_fusion.11), channel_id=1, source_target_pairs={{0,16},{4,20},{8,24},{12,28},{16,0},{20,4},{24,8},{28,12},{1,17},{... | collective-permute-start | bytes 221192 | tf_op jit(solution)/shard_map/ppermute | solution.py:543
  393.9 23.5 %copy-start.23 = (f32[24]{0:T(128)S(1)}, f32[24]{0:T(128)}, u32[]{:S(2)}) copy-start(f32[24]{0:T(128)} %reduce_sum.110) | copy-start | bytes 292
  393.9 13.5 %collective-permute-start.21 = (bf16[48,768]{1,0:T(8,128)(2,1)S(1)}, bf16[48,768]{1,0:T(8,128)(2,1)S(1)}, u32[]{:S(2)}, u32[]{:S(2)}) collective-permute-start(bf16[48,768]{1,0:T(8,128)(2,1)S(1)} %dynamic-slice_bitcast_fusion.10), channel_id=1, source_target_pairs={{0,16},{4,20},{8,24},{12,28},{16,0},{20,4},{24,8},{28,12},{1,17},{... | collective-permute-start | bytes 221192 | tf_op jit(solution)/shard_map/ppermute | solution.py:543
  401.1 29.7 %copy-start.24 = (f32[128]{0:T(128)S(1)}, f32[128]{0:T(128)}, u32[]{:S(2)}) copy-start(f32[128]{0:T(128)} %param.30) | copy-start | bytes 1540
  401.1 29.7 %copy-start.25 = (f32[128]{0:T(128)S(1)}, f32[128]{0:T(128)}, u32[]{:S(2)}) copy-start(f32[128]{0:T(128)} %param.32) | copy-start | bytes 1540
  401.1 29.7 %copy-start.26 = (f32[128]{0:T(128)S(1)}, f32[128]{0:T(128)}, u32[]{:S(2)}) copy-start(f32[128]{0:T(128)} %param.31) | copy-start | bytes 1540
  401.2 30.3 %copy-start.4 = (f32[24,3352]{1,0:T(8,128)S(1)}, f32[24,3352]{1,0:T(8,128)}, u32[]{:S(2)}) copy-start(f32[24,3352]{1,0:T(8,128)} %param.21) | copy-start | bytes 965380
  401.2 30.3 %copy-start.7 = (f32[24,3352]{1,0:T(8,128)S(1)}, f32[24,3352]{1,0:T(8,128)}, u32[]{:S(2)}) copy-start(f32[24,3352]{1,0:T(8,128)} %param.23) | copy-start | bytes 965380
  401.2 30.3 %copy-start.8 = (f32[24,3352]{1,0:T(8,128)S(1)}, f32[24,3352]{1,0:T(8,128)}, u32[]{:S(2)}) copy-start(f32[24,3352]{1,0:T(8,128)} %param.22) | copy-start | bytes 965380
  401.2 5.8 %collective-permute-start.15 = (bf16[2,24,1920]{2,1,0:T(8,128)(2,1)S(1)}, bf16[2,24,1920]{2,1,0:T(8,128)(2,1)S(1)}, u32[]{:S(2)}, u32[]{:S(2)}) collective-permute-start(bf16[2,24,1920]{2,1,0:T(8,128)(2,1)S(1)} %dynamic-slice_bitcast_fusion.6), channel_id=1, source_target_pairs={{0,8},{4,12},{8,0},{12,4},{16,24},{20,28},{24,16},{28,20},{1,9},{5... | collective-permute-start | bytes 552968 | tf_op jit(solution)/shard_map/ppermute | solution.py:543
  407.1 5.5 %collective-permute-start.16 = (bf16[24,1920]{1,0:T(8,128)(2,1)S(1)}, bf16[24,1920]{1,0:T(8,128)(2,1)S(1)}, u32[]{:S(2)}, u32[]{:S(2)}) collective-permute-start(bf16[24,1920]{1,0:T(8,128)(2,1)S(1)} %dynamic-slice_bitcast_fusion.9), channel_id=1, source_target_pairs={{0,16},{4,20},{8,24},{12,28},{16,0},{20,4},{24,8},{28,12},{1,17},{... | collective-permute-start | bytes 276488 | tf_op jit(solution)/shard_map/ppermute | solution.py:543
  414.7 17.9 %copy-start.18 = (f32[3,24]{1,0:T(4,128)S(1)}, f32[3,24]{1,0:T(4,128)}, u32[]{:S(2)}) copy-start(f32[3,24]{1,0:T(4,128)} %param.33) | copy-start | bytes 868
  414.7 17.9 %copy-start.19 = (f32[3,24]{1,0:T(4,128)S(1)}, f32[3,24]{1,0:T(4,128)}, u32[]{:S(2)}) copy-start(f32[3,24]{1,0:T(4,128)} %param.35) | copy-start | bytes 868
  414.7 17.9 %copy-start.20 = (f32[3,24]{1,0:T(4,128)S(1)}, f32[3,24]{1,0:T(4,128)}, u32[]{:S(2)}) copy-start(f32[3,24]{1,0:T(4,128)} %param.34) | copy-start | bytes 868
  414.7 18.5 %copy-start.15 = (f32[4,56]{1,0:T(4,128)S(1)}, f32[4,56]{1,0:T(4,128)}, u32[]{:S(2)}) copy-start(f32[4,56]{1,0:T(4,128)} %param.27) | copy-start | bytes 2692
  414.7 18.5 %copy-start.21 = (f32[4,56]{1,0:T(4,128)S(1)}, f32[4,56]{1,0:T(4,128)}, u32[]{:S(2)}) copy-start(f32[4,56]{1,0:T(4,128)} %param.29) | copy-start | bytes 2692
  414.8 18.5 %copy-start.22 = (f32[4,56]{1,0:T(4,128)S(1)}, f32[4,56]{1,0:T(4,128)}, u32[]{:S(2)}) copy-start(f32[4,56]{1,0:T(4,128)} %param.28) | copy-start | bytes 2692
  417.5 16.4 %copy-start.5 = (f32[48,768]{1,0:T(8,128)S(1)}, f32[48,768]{1,0:T(8,128)}, u32[]{:S(2)}) copy-start(f32[48,768]{1,0:T(8,128)} %param.24) | copy-start | bytes 442372
  417.5 16.4 %copy-start.9 = (f32[48,768]{1,0:T(8,128)S(1)}, f32[48,768]{1,0:T(8,128)}, u32[]{:S(2)}) copy-start(f32[48,768]{1,0:T(8,128)} %param.26) | copy-start | bytes 442372
  417.5 16.4 %copy-start.10 = (f32[48,768]{1,0:T(8,128)S(1)}, f32[48,768]{1,0:T(8,128)}, u32[]{:S(2)}) copy-start(f32[48,768]{1,0:T(8,128)} %param.25) | copy-start | bytes 442372
  430.8 4.0 copy-start.16
  430.8 4.0 copy-start.14
Sparse Core Ops, SparseCore 0:
  11.5 61.3 all-gather.2
  76.4 57.2 all-gather.4
